TPU v7x, 32 devices: a whole 2x2x4 slice. The times are simulated.
32 devices in a mesh: ctx: 8 (over y, x, core), tp: 4 (over z).
Axes of the slice: x: 2, y: 2, z: 4, core: 2. Of those that a mesh axis runs over, the one named last changes fastest.
Arguments:
- queries: bfloat16 [2, 8, 128, 8192], P(None, 'ctx', None, 'tp'), may hold values from -5 to 5
- keys: bfloat16 [2, 8, 128, 1024], P(None, 'ctx', None, 'tp'), may hold values from -5 to 5
- values: bfloat16 [2, 8, 128, 1024], P(None, 'ctx', None, 'tp'), may hold values from -6 to 6
- out_grad: bfloat16 [2, 8, 128, 8192], P(None, 'ctx', None, 'tp'), may hold values from -6 to 6
- block_doc: int32 [16], replicated, may hold values from 0 to 15, as said below
Outputs:
- attn_out: bfloat16 [2, 8, 128, 8192], P(None, 'ctx', None, 'tp')
- query_grad: bfloat16 [2, 8, 128, 8192], P(None, 'ctx', None, 'tp')
- key_grad: bfloat16 [2, 8, 128, 1024], P(None, 'ctx', None, 'tp')
- value_grad: bfloat16 [2, 8, 128, 1024], P(None, 'ctx', None, 'tp')
Inputs may be any that keep to these rules, and one draw needn't show every extreme that they name: block_doc never falls along the sequence; each document covers 1 to 2 consecutive blocks, and in each half of the sequence the first document covers exactly 2; no document holds both block 7 and block 8; the first block's id is 0 and the last block's id is 15.
All inputs are finite; a program needn't handle non-finite values.
Results may differ from a plain program's by a relative error of at most 0.0094.
Values may be sent and summed in bfloat16 or wider, within the bound.
No kernel may reach another device: no remote copies, remote signals or barrier semaphores. Data moves between devices by JAX's collectives and lax.ppermute only.
A program may use at most 64 MiB of HBM per device.

v0:
```python
import math

import jax
import jax.numpy as jnp
from jax import lax
from jax.sharding import PartitionSpec as P

HQ = 64
HK = 8
HD = 128
BLOCK = 128


masked_score = -1e30


def shifted(block, axis, distance):
    devices = range(lax.axis_size(axis))
    route = [(i - distance, i) for i in devices if i - distance in devices]
    return lax.ppermute(block, axis, route)


def move_keys(payload, distance):
    return shifted(payload, "ctx", distance)


def move_grads(payload, distance):
    return shifted(payload.astype(jnp.bfloat16), "ctx", distance).astype(payload.dtype)


def piece_docs(block_doc, piece_index, piece_len):
    per_piece = piece_len // BLOCK
    start = jnp.maximum(piece_index, 0) * per_piece
    doc_blocks = lax.dynamic_slice_in_dim(block_doc, start, per_piece, 0)
    doc_tokens = jnp.repeat(doc_blocks, BLOCK)
    return jnp.where(piece_index >= 0, doc_tokens, -1)


def attend(query_piece, grad_piece, key_buffer, piece_index, block_doc):
    window, _, piece_len, features = key_buffer.shape
    kv_heads = features // HD
    scaling = 1.0 / math.sqrt(HD)
    key_slots = key_buffer[:, 0].reshape(window, piece_len, kv_heads, HD)
    value_slots = key_buffer[:, 1].reshape(window, piece_len, kv_heads, HD)
    keys_flat = key_slots.reshape(window * piece_len, kv_heads, HD)
    values_flat = value_slots.reshape(window * piece_len, kv_heads, HD)
    positions = jnp.arange(piece_len, dtype=jnp.int32)
    query_docs = piece_docs(block_doc, piece_index, piece_len)
    query_pos = piece_index * piece_len + positions
    visible_rows = []
    for slot_index in range(window):
        key_index = piece_index - (window - 1) + slot_index
        key_docs = piece_docs(block_doc, key_index, piece_len)
        key_pos = key_index * piece_len + positions
        visible_rows.append(
            (key_docs[None, :] == query_docs[:, None]) & (key_pos[None, :] <= query_pos[:, None])
        )
    visible = jnp.concatenate(visible_rows, axis=1)

    def key_side(form, left, flat):
        return jnp.einsum(form, left, flat, preferred_element_type=jnp.float32)

    def key_sum(form, weights, flat):
        return jnp.einsum(form, weights, flat, preferred_element_type=jnp.float32)

    def per_key(form, weights, right):
        return jnp.einsum(form, weights, right, preferred_element_type=jnp.float32).reshape(
            window, piece_len, kv_heads, HD
        )

    raw_scores = key_side("qhgd,khd->hgqk", query_piece, keys_flat)
    scores = jnp.where(visible[None, None], raw_scores * scaling, masked_score)
    row_max = jnp.max(scores, axis=-1, keepdims=True)
    log_total = row_max + jnp.log(jnp.sum(jnp.exp(scores - row_max), axis=-1, keepdims=True))
    probs = jnp.exp(scores - log_total)
    probs_low = probs.astype(jnp.bfloat16)
    attended = key_sum("hgqk,khd->qhgd", probs_low, values_flat)
    out_low = attended.astype(jnp.bfloat16)
    out_back = lax.optimization_barrier(out_low).astype(jnp.float32)
    delta = jnp.einsum("qhgd,qhgd->hgq", grad_piece.astype(jnp.float32), out_back)
    dprobs = key_side("qhgd,khd->hgqk", grad_piece, values_flat)
    dscores = (probs * (dprobs - delta[..., None])).astype(jnp.bfloat16)
    query_part = (key_sum("hgqk,khd->qhgd", dscores, keys_flat) * scaling).astype(jnp.bfloat16)
    key_part = per_key("hgqk,qhgd->khd", dscores, query_piece) * scaling
    value_part = per_key("hgqk,qhgd->khd", probs_low, grad_piece)
    grads = jnp.stack(
        [
            key_part.reshape(window, piece_len, features),
            value_part.reshape(window, piece_len, features),
        ],
        axis=1,
    )
    return (out_low.reshape(piece_len, -1), query_part.reshape(piece_len, -1), grads)


def local(queries, keys, values, out_grad, block_doc):
    ctx_size = lax.axis_size("ctx")
    my_index = lax.axis_index("ctx")
    reach_back = min(7, ctx_size // 4 - 1)
    window = reach_back + 1
    levels = window.bit_length() - 1
    piece_len = queries.shape[2]
    kv_heads = keys.shape[3] // HD
    group = HQ // HK
    query_all = queries[:, 0].reshape(2, piece_len, kv_heads, group, HD)
    grad_all = out_grad[:, 0].reshape(2, piece_len, kv_heads, group, HD)
    paired = jnp.stack([keys[:, 0], values[:, 0]], axis=1)
    low_buffer = paired[0][None]
    high_buffer = paired[1][None]
    for level_bit in range(levels):
        distance = 1 << level_bit
        low_buffer = jnp.concatenate([move_keys(low_buffer, distance), low_buffer], axis=0)
        high_buffer = jnp.concatenate([move_keys(high_buffer, -distance), high_buffer], axis=0)
    high_index = 2 * ctx_size - 1 - my_index
    low_out, low_qgrad, low_grads = attend(
        query_all[0], grad_all[0], low_buffer, my_index, block_doc
    )
    high_out, high_qgrad, high_grads = attend(
        query_all[1], grad_all[1], high_buffer, high_index, block_doc
    )
    low_back = low_grads
    high_back = high_grads
    for level_bit in reversed(range(levels)):
        distance = 1 << level_bit
        low_back = low_back[distance:] + move_grads(low_back[:distance], -distance)
        high_back = high_back[distance:] + move_grads(high_back[:distance], distance)
    low_total = low_back[0]
    high_total = high_back[0]
    attn_pair = jnp.stack([low_out, high_out])[:, None]
    qgrad_pair = jnp.stack([low_qgrad, high_qgrad])[:, None]
    key_pair = jnp.stack([low_total[0], high_total[0]]).astype(jnp.bfloat16)[:, None]
    value_pair = jnp.stack([low_total[1], high_total[1]]).astype(jnp.bfloat16)[:, None]
    return (attn_pair, qgrad_pair, key_pair, value_pair)


def solution(mesh):
    in_specs = (
        P(None, "ctx", None, "tp"),
        P(None, "ctx", None, "tp"),
        P(None, "ctx", None, "tp"),
        P(None, "ctx", None, "tp"),
        P(),
    )
    out_specs = (
        P(None, "ctx", None, "tp"),
        P(None, "ctx", None, "tp"),
        P(None, "ctx", None, "tp"),
        P(None, "ctx", None, "tp"),
    )
    return jax.shard_map(local, mesh=mesh, in_specs=in_specs, out_specs=out_specs, check_vma=False)
```

profile of v0, /device:TPU:27, one launch (start us, length us, event | category | flops | bytes accessed | tf_op | source)
XLA Modules:
  0.0 43.6 jit_solution(4134720101621341771)
XLA Ops:
  0.6 0.9 %constant_dynamic-update-slice_fusion.1 = bf16[2,2,128,256]{3,2,1,0:T(8,128)(2,1)S(1)} fusion(bf16[2,1,128,256]{3,2,1,0:T(8,128)(2,1)} %param.6), kind=kLoop, calls=%fused_computation.61 | loop fusion | bytes 262144
  1.5 0.9 %constant_dynamic-update-slice_fusion = bf16[2,2,128,256]{3,2,1,0:T(8,128)(2,1)S(1)} fusion(bf16[2,2,128,256]{3,2,1,0:T(8,128)(2,1)S(1)} %constant_dynamic-update-slice_fusion.1, bf16[2,1,128,256]{3,2,1,0:T(8,128)(2,1)} %param.7), kind=kLoop, calls=%fused_computation.60 | loop fusion | bytes 262144 | tf_op jit(solution)/shard_map/stack | solution.py:107
  2.5 3.7 %collective-permute-start = (bf16[1,2,128,256]{3,2,1,0:T(8,128)(2,1)S(1)}, bf16[1,2,128,256]{3,2,1,0:T(8,128)(2,1)}, u32[]{:S(2)}, u32[]{:S(2)}) collective-permute-start(bf16[1,2,128,256]{3,2,1,0:T(8,128)(2,1)S(1)} %get-tuple-element.14), channel_id=1, source_target_pairs={{0,4},{4,8},{8,12},{12,16},{16,20},{20,24},{24,28},{1,5},{5,9},{9,... | collective-permute-start | bytes 393224 | tf_op jit(solution)/shard_map/ppermute | solution.py:20
  6.2 1.9 %collective-permute-start.1 = (bf16[1,2,128,256]{3,2,1,0:T(8,128)(2,1)S(1)}, bf16[1,2,128,256]{3,2,1,0:T(8,128)(2,1)}, u32[]{:S(2)}, u32[]{:S(2)}) collective-permute-start(bf16[1,2,128,256]{3,2,1,0:T(8,128)(2,1)S(1)} %get-tuple-element.15), channel_id=1, source_target_pairs={{4,0},{8,4},{12,8},{16,12},{20,16},{24,20},{28,24},{5,1},{9,5},{13... | collective-permute-start | bytes 393224 | tf_op jit(solution)/shard_map/ppermute | solution.py:20
  8.2 1.4 %fusion.27 = (bf16[1,1,128,2048]{3,2,1,0:T(8,128)(2,1)S(1)}, bf16[1,1,128,2048]{3,2,1,0:T(8,128)(2,1)S(1)}) fusion(bf16[2,1,128,2048]{3,2,1,0:T(8,128)(2,1)} %param.5), kind=kLoop, calls=%fused_computation.73 | loop fusion | bytes 2097152 | tf_op jit(solution)/shard_map/slice | solution.py:116
  9.8 0.6 %fusion.31 = (s32[1]{0:T(128)}, s32[1]{0:T(128)}, s32[1]{0:T(128)}, s32[1]{0:T(128)}) fusion(s32[16]{0:T(128)S(1)} %copy-done.5, s32[]{:T(128)S(6)} %max.15, s32[]{:T(128)S(6)} %max.14, s32[]{:T(128)S(6)} %max.17, s32[]{:T(128)S(6)} %max.16), kind=kLoop, calls=%fused_computation.77 | loop fusion | bytes 48 | tf_op jit(solution)/shard_map/dynamic_slice | solution.py:34
  13.2 0.6 %pad_add_fusion.1 = pred[128,256]{0,1:T(8,128)(4,1)} fusion(pred[128,128]{0,1:T(8,128)(4,1)S(1)} %get-tuple-element.29, pred[128,128]{0,1:T(8,128)(4,1)S(1)} %get-tuple-element.28), kind=kLoop, calls=%fused_computation.55 | loop fusion | flops 32768 | bytes 65536 | tf_op jit(solution)/shard_map/concatenate | solution.py:58
  15.0 0.6 %pad_add_fusion = pred[128,256]{0,1:T(8,128)(4,1)} fusion(pred[128,128]{0,1:T(8,128)(4,1)S(1)} %get-tuple-element.23, pred[128,128]{0,1:T(8,128)(4,1)S(1)} %get-tuple-element.22), kind=kLoop, calls=%fused_computation.54 | loop fusion | flops 32768 | bytes 65536 | tf_op jit(solution)/shard_map/concatenate | solution.py:58
  15.6 0.9 %fusion.20 = (bf16[2,1,128,256]{3,2,1,0:T(8,128)(2,1)S(1)}, bf16[2,1,128,256]{3,2,1,0:T(8,128)(2,1)S(1)}) fusion(bf16[1,2,128,256]{3,2,1,0:T(8,128)(2,1)} %collective-permute-done.1, bf16[1,2,128,256]{3,2,1,0:T(8,128)(2,1)S(1)} %get-tuple-element.15), kind=kLoop, calls=%fused_computation.44 | loop fusion | flops 131072 | bytes 524288 | tf_op jit(solution)/shard_map/concatenate | solution.py:113
  16.8 1.3 %fusion.32 = (f32[2,8,128]{2,1,0:T(8,128)S(1)}, f32[2,8,128,256]{2,3,1,0:T(8,128)S(1)}) fusion(bf16[256,2,128,1]{0,2,3,1:T(8,128)(2,1)S(1)} %copy.83, bf16[128,2,8,128]{0,3,2,1:T(8,128)(2,1)S(1)} %bitcast.128, pred[128,256]{0,1:T(8,128)(4,1)} %pad_add_fusion.1), kind=kOutput, calls=%fused_computation.78 | convolution fusion | flops 135788544 | bytes 2793472 | tf_op jit(solution)/shard_map/qhgd,khd->hgqk/dot_general | solution.py:61
  19.1 0.6 %fusion.1 = bf16[2,8,128,256]{2,3,1,0:T(8,128)(2,1)S(1)} fusion(f32[2,8,128,256]{2,3,1,0:T(8,128)S(1)} %get-tuple-element.31, bf16[128,2,8,128]{0,3,2,1:T(8,128)(2,1)S(1)} %bitcast.124, f32[2,8,128]{2,1,0:T(8,128)S(1)} %fusion.12, f32[2,8,128]{2,1,0:T(8,128)S(1)} %log_add_fusion, bf16[256,2,128,1]{2,1,0,3:T(2,128)(2,1)S(1)} %bitcast.137), kind=kOutput, calls=%fused_computation.2 | convolution fusion | flops 136314880 | bytes 3817472 | tf_op jit(solution)/shard_map/qhgd,khd->hgqk/dot_general | solution.py:61
  20.4 1.2 %convolution_bitcast_fusion = f32[256,2,128]{2,0,1:T(8,128)} fusion(bf16[128,2,8,128]{0,3,2,1:T(8,128)(2,1)S(1)} %bitcast.125, f32[2,8,128,256]{2,3,1,0:T(8,128)S(1)} %get-tuple-element.31, f32[2,8,128]{2,1,0:T(8,128)S(1)} %log_add_fusion), kind=kOutput, calls=%fused_computation.20 | convolution fusion | flops 135266304 | bytes 2891776 | tf_op jit(solution)/shard_map/hgqk,qhgd->khd/dot_general | solution.py:67
  21.6 0.9 %fusion.21 = (bf16[2,1,128,256]{3,2,1,0:T(8,128)(2,1)S(1)}, bf16[2,1,128,256]{3,2,1,0:T(8,128)(2,1)S(1)}) fusion(bf16[1,2,128,256]{3,2,1,0:T(8,128)(2,1)} %collective-permute-done, bf16[1,2,128,256]{3,2,1,0:T(8,128)(2,1)S(1)} %get-tuple-element.14), kind=kLoop, calls=%fused_computation.45 | loop fusion | flops 131072 | bytes 524288 | tf_op jit(solution)/shard_map/concatenate | solution.py:112
  23.6 1.2 %convolution_bitcast_fusion.2 = f32[256,2,128]{2,0,1:T(8,128)} fusion(bf16[128,2,8,128]{0,3,2,1:T(8,128)(2,1)S(1)} %bitcast.120, f32[2,8,128,256]{2,3,1,0:T(8,128)S(1)} %get-tuple-element.33, f32[2,8,128]{2,1,0:T(8,128)S(1)} %log_add_fusion.1), kind=kOutput, calls=%fused_computation.24 | convolution fusion | flops 135266304 | bytes 2891776 | tf_op jit(solution)/shard_map/hgqk,qhgd->khd/dot_general | solution.py:67
  25.5 0.6 %fusion.3 = bf16[2,8,128,256]{2,3,1,0:T(8,128)(2,1)S(1)} fusion(f32[2,8,128,256]{2,3,1,0:T(8,128)S(1)} %get-tuple-element.33, bf16[128,2,8,128]{0,3,2,1:T(8,128)(2,1)S(1)} %bitcast.122, f32[2,8,128]{2,1,0:T(8,128)S(1)} %fusion.13, f32[2,8,128]{2,1,0:T(8,128)S(1)} %log_add_fusion.1, bf16[256,2,128,1]{2,1,0,3:T(2,128)(2,1)S(1)} %bitcast.136), kind=kOutput, calls=%fused_computation.5 | convolution fusion | flops 136314880 | bytes 3817472 | tf_op jit(solution)/shard_map/qhgd,khd->hgqk/dot_general | solution.py:61
  28.1 4.5 %collective-permute-start.3 = (bf16[1,2,128,256]{3,2,0,1:T(8,128)(2,1)S(1)}, bf16[1,2,128,256]{3,2,0,1:T(8,128)(2,1)}, u32[]{:S(2)}, u32[]{:S(2)}) collective-permute-start(bf16[1,2,128,256]{3,2,0,1:T(8,128)(2,1)S(1)} %slice.120), channel_id=1, source_target_pairs={{0,4},{4,8},{8,12},{12,16},{16,20},{20,24},{24,28},{1,5},{5,9},{9,... | collective-permute-start | bytes 393224 | tf_op jit(solution)/shard_map/ppermute | solution.py:20
  32.9 1.2 %copy.50 = f32[256,2,128]{2,1,0:T(2,128)S(1)} copy(f32[256,2,128]{2,0,1:T(8,128)} %convolution_bitcast_fusion.2) | data formatting | bytes 524288 | tf_op jit(solution)/shard_map/hgqk,qhgd->khd/transpose | solution.py:67
  35.0 1.9 %collective-permute-start.2 = (bf16[1,2,128,256]{3,2,0,1:T(8,128)(2,1)S(1)}, bf16[1,2,128,256]{3,2,0,1:T(8,128)(2,1)S(1)}, u32[]{:S(2)}, u32[]{:S(2)}) collective-permute-start(bf16[1,2,128,256]{3,2,0,1:T(8,128)(2,1)S(1)} %slice.121), channel_id=1, source_target_pairs={{4,0},{8,4},{12,8},{16,12},{20,16},{24,20},{28,24},{5,1},{9,5},{13... | collective-permute-start | bytes 393224 | tf_op jit(solution)/shard_map/ppermute | solution.py:20
  37.2 1.1 %maximum_bitcast_fusion.1 = bf16[2,1,128,2048]{3,2,1,0:T(8,128)(2,1)} fusion(bf16[1,128,2048]{2,1,0:T(8,128)(2,1)S(1)} %copy.46, bf16[1,128,2048]{2,1,0:T(8,128)(2,1)S(1)} %copy.45), kind=kLoop, calls=%fused_computation.29 | loop fusion | flops 524288 | bytes 2097152 | tf_op jit(solution)/shard_map/broadcast_in_dim | solution.py:130
  38.3 1.1 %maximum_bitcast_fusion = bf16[2,1,128,2048]{3,2,1,0:T(8,128)(2,1)} fusion(bf16[1,128,2048]{2,1,0:T(8,128)(2,1)S(1)} %copy.34, bf16[1,128,2048]{2,1,0:T(8,128)(2,1)S(1)} %copy.33), kind=kLoop, calls=%fused_computation.28 | loop fusion | flops 524288 | bytes 2097152 | tf_op jit(solution)/shard_map/broadcast_in_dim | solution.py:129
  39.3 0.9 %fusion.18 = bf16[1,2,128,256]{3,2,0,1:T(8,128)(2,1)S(1)} fusion(f32[2,2,128,256]{3,2,0,1:T(8,128)S(1)} %copy-done.3, bf16[1,2,128,256]{3,2,0,1:T(8,128)(2,1)} %collective-permute-done.3), kind=kLoop, calls=%fused_computation.36 | loop fusion | flops 196608 | bytes 524288 | tf_op jit(solution)/shard_map/convert.6
  40.3 1.9 %collective-permute-done.2 = bf16[1,2,128,256]{3,2,0,1:T(8,128)(2,1)S(1)} collective-permute-done((bf16[1,2,128,256]{3,2,0,1:T(8,128)(2,1)S(1)}, bf16[1,2,128,256]{3,2,0,1:T(8,128)(2,1)S(1)}, u32[]{:S(2)}, u32[]{:S(2)}) %collective-permute-start.2) | collective-permute-done | bytes 131104 | tf_op jit(solution)/shard_map/ppermute | solution.py:20
  42.3 0.7 %maximum_bitcast_fusion.3 = bf16[2,1,128,256]{3,2,1,0:T(8,128)(2,1)} fusion(bf16[1,1,128,256]{3,2,0,1:T(8,128)(2,1)S(1)} %get-tuple-element.20, bf16[1,1,128,256]{3,2,0,1:T(8,128)(2,1)S(1)} %get-tuple-element.18), kind=kLoop, calls=%fused_computation.49 | loop fusion | flops 65536 | bytes 262144
  42.9 0.7 %maximum_bitcast_fusion.2 = bf16[2,1,128,256]{3,2,1,0:T(8,128)(2,1)} fusion(bf16[1,1,128,256]{3,2,0,1:T(8,128)(2,1)S(1)} %get-tuple-element.21, bf16[1,1,128,256]{3,2,0,1:T(8,128)(2,1)S(1)} %get-tuple-element.19), kind=kLoop, calls=%fused_computation.48 | loop fusion | flops 65536 | bytes 262144
  (66 shorter events, 8.8 us)
Async XLA Ops:
  2.5 19.1 %collective-permute-start = (bf16[1,2,128,256]{3,2,1,0:T(8,128)(2,1)S(1)}, bf16[1,2,128,256]{3,2,1,0:T(8,128)(2,1)}, u32[]{:S(2)}, u32[]{:S(2)}) collective-permute-start(bf16[1,2,128,256]{3,2,1,0:T(8,128)(2,1)S(1)} %get-tuple-element.14), channel_id=1, source_target_pairs={{0,4},{4,8},{8,12},{12,16},{16,20},{20,24},{24,28},{1,5},{5,9},{9,... | collective-permute-start | bytes 393224 | tf_op jit(solution)/shard_map/ppermute | solution.py:20
  6.2 9.4 %collective-permute-start.1 = (bf16[1,2,128,256]{3,2,1,0:T(8,128)(2,1)S(1)}, bf16[1,2,128,256]{3,2,1,0:T(8,128)(2,1)}, u32[]{:S(2)}, u32[]{:S(2)}) collective-permute-start(bf16[1,2,128,256]{3,2,1,0:T(8,128)(2,1)S(1)} %get-tuple-element.15), channel_id=1, source_target_pairs={{4,0},{8,4},{12,8},{16,12},{20,16},{24,20},{28,24},{5,1},{9,5},{13... | collective-permute-start | bytes 393224 | tf_op jit(solution)/shard_map/ppermute | solution.py:20
  8.1 1.5 %copy-start = (bf16[2,1,128,2048]{3,2,1,0:T(8,128)(2,1)S(1)}, bf16[2,1,128,2048]{3,2,1,0:T(8,128)(2,1)}, u32[]{:S(2)}) copy-start(bf16[2,1,128,2048]{3,2,1,0:T(8,128)(2,1)} %param.8) | copy-start | bytes 3145732
  8.1 1.6 %copy-start.5 = (s32[16]{0:T(128)S(1)}, s32[16]{0:T(128)}, u32[]{:S(2)}) copy-start(s32[16]{0:T(128)} %param.9) | copy-start | bytes 196
  20.4 2.4 %copy-start.4 = (pred[128,256]{0,1:T(8,128)(4,1)S(1)}, pred[128,256]{0,1:T(8,128)(4,1)}, u32[]{:S(2)}) copy-start(pred[128,256]{0,1:T(8,128)(4,1)} %pad_add_fusion) | copy-start | bytes 98308
  26.0 1.0 %copy-start.1 = (f32[256,2,128]{2,0,1:T(8,128)S(1)}, f32[256,2,128]{2,0,1:T(8,128)}, u32[]{:S(2)}) copy-start(f32[256,2,128]{2,0,1:T(8,128)} %convolution_bitcast_fusion) | copy-start | bytes 786436
  28.1 4.6 %copy-start.2 = (f32[2,2,128,256]{3,2,0,1:T(8,128)}, f32[2,2,128,256]{3,2,0,1:T(8,128)S(1)}, u32[]{:S(2)}) copy-start(f32[2,2,128,256]{3,2,0,1:T(8,128)S(1)} %constant_dynamic-update-slice_fusion.4) | copy-start | bytes 1572868
  28.1 11.2 %collective-permute-start.3 = (bf16[1,2,128,256]{3,2,0,1:T(8,128)(2,1)S(1)}, bf16[1,2,128,256]{3,2,0,1:T(8,128)(2,1)}, u32[]{:S(2)}, u32[]{:S(2)}) collective-permute-start(bf16[1,2,128,256]{3,2,0,1:T(8,128)(2,1)S(1)} %slice.120), channel_id=1, source_target_pairs={{0,4},{4,8},{8,12},{12,16},{16,20},{20,24},{24,28},{1,5},{5,9},{9,... | collective-permute-start | bytes 393224 | tf_op jit(solution)/shard_map/ppermute | solution.py:20
  35.0 7.2 %collective-permute-start.2 = (bf16[1,2,128,256]{3,2,0,1:T(8,128)(2,1)S(1)}, bf16[1,2,128,256]{3,2,0,1:T(8,128)(2,1)S(1)}, u32[]{:S(2)}, u32[]{:S(2)}) collective-permute-start(bf16[1,2,128,256]{3,2,0,1:T(8,128)(2,1)S(1)} %slice.121), channel_id=1, source_target_pairs={{4,0},{8,4},{12,8},{16,12},{20,16},{24,20},{28,24},{5,1},{9,5},{13... | collective-permute-start | bytes 393224 | tf_op jit(solution)/shard_map/ppermute | solution.py:20
  37.2 2.1 %copy-start.3 = (f32[2,2,128,256]{3,2,0,1:T(8,128)S(1)}, f32[2,2,128,256]{3,2,0,1:T(8,128)}, u32[]{:S(2)}) copy-start(f32[2,2,128,256]{3,2,0,1:T(8,128)} %copy-done.2) | copy-start | bytes 1572868
where the time goes:
time: 44.1 us; the launch traced here: 43.6 us
  starting transfers between devices  12.1 us (27%)
  local copies, waits for them, and re-layouts  9.55 us (22%)
  other arithmetic  8.62 us (20%)
  matrix products  7.67 us (17%)
  between operations  3.74 us (8%)
  waiting for transfers between devices  1.95 us (4%)
    ppermute x4, starting transfers between devices, shifted(): return lax.ppermute(block, axis, route)  12.1 us
    dot_general x4, matrix products, per_key(): jnp.einsum(form, weights, right, preferred_element_type=jnp.float32)  3.18 us
    dot_general x4, matrix products, key_side(): return jnp.einsum(form, left, flat, preferred_element_type=jnp.float32)  2.86 us
    unnamed x19, local copies, waits for them, and re-layouts  2.41 us
    ppermute x4, waiting for transfers between devices, shifted(): return lax.ppermute(block, axis, route)  1.95 us
    dot_general x4, matrix products, key_sum(): return jnp.einsum(form, weights, flat, preferred_element_type=jnp.float32)  1.63 us
    transpose x2, local copies, waits for them, and re-layouts, per_key(): jnp.einsum(form, weights, right, preferred_element_type=jnp.float32)  1.36 us
    slice x1, local copies, waits for them, and re-layouts, local(): query_all[0]  1.36 us
  transfers between devices with their start and end apart: 4, of which 1 were waited for; matrix products, arithmetic and copies ran while one was open for 37% of the time, Pallas kernels for 0%

commit v1 on v0

--- a/solution.py
+++ b/solution.py
@@ -3,6 +3,8 @@
 import jax
 import jax.numpy as jnp
 from jax import lax
+from jax.experimental import pallas as pl
+from jax.experimental.pallas import tpu as pltpu
 from jax.sharding import PartitionSpec as P
 
 HQ = 64
@@ -93,7 +95,7 @@
     return (out_low.reshape(piece_len, -1), query_part.reshape(piece_len, -1), grads)
 
 
-def local(queries, keys, values, out_grad, block_doc):
+def local_wide(queries, keys, values, out_grad, block_doc):
     ctx_size = lax.axis_size("ctx")
     my_index = lax.axis_index("ctx")
     reach_back = min(7, ctx_size // 4 - 1)
@@ -133,6 +135,381 @@
     return (attn_pair, qgrad_pair, key_pair, value_pair)
 
 
+GROUP = HQ // HK
+CHUNK = 2 * HD
+LOG2_SCALE = math.log2(math.e) / math.sqrt(HD)
+SCALE = 1.0 / math.sqrt(HD)
+VMEM_LIMIT = 24 * 1024 * 1024
+
+F32 = jnp.float32
+BF16 = jnp.bfloat16
+
+in_vmem = pl.BlockSpec(memory_space=pltpu.VMEM)
+in_hbm = pl.BlockSpec(memory_space=pltpu.HBM)
+in_smem = pl.BlockSpec(memory_space=pltpu.SMEM)
+
+
+def dot(left, right):
+    return jnp.dot(left, right, preferred_element_type=F32)
+
+
+def dot_t(left, right):
+    return lax.dot_general(left, right, (((1,), (1,)), ((), ())), preferred_element_type=F32)
+
+
+def near_slot():
+    return lax.rem(lax.axis_index("ctx"), 2)
+
+
+def far_slot():
+    return 1 - near_slot()
+
+
+def linked(doc_ref, slot):
+    pairs = lax.axis_size("ctx")
+    me = lax.axis_index("ctx")
+    piece = jnp.where(slot == 0, me, 2 * pairs - 1 - me)
+    same = doc_ref[piece] == doc_ref[jnp.maximum(piece - 1, 0)]
+    return jnp.where(jnp.logical_and(piece > 0, same), 0.0, masked_score).astype(F32)
+
+
+def lanes(ref, first, count):
+    parts = [ref[:, pl.ds(first + i * HD, HD)] for i in range(count)]
+    return jnp.concatenate(parts, axis=0)
+
+
+def causal(rows, columns):
+    key = lax.broadcasted_iota(jnp.int32, (rows, columns), 0)
+    query = lax.broadcasted_iota(jnp.int32, (rows, columns), 1)
+    return key <= lax.rem(query, rows)
+
+
+def fetch_pairs(pairs_of_refs, sems):
+    copies = [pltpu.make_async_copy(a, b, sems.at[i]) for i, (a, b) in enumerate(pairs_of_refs)]
+    for copy in copies:
+        copy.start()
+    return copies
+
+
+def pick_kernel(keys, values, far_kv, near_kv, sems):
+    far, near = far_slot(), near_slot()
+    copies = fetch_pairs(
+        [
+            (keys.at[far, 0], far_kv.at[0]),
+            (values.at[far, 0], far_kv.at[1]),
+            (keys.at[near, 0], near_kv.at[0]),
+            (values.at[near, 0], near_kv.at[1]),
+        ],
+        sems,
+    )
+    for copy in copies:
+        copy.wait()
+
+
+def pick(keys, values):
+    _, _, piece_len, features = keys.shape
+    shape = pltpu.VMEM((2, piece_len, features), BF16)
+    return pl.pallas_call(
+        pick_kernel,
+        out_shape=(shape, shape),
+        in_specs=[in_hbm, in_hbm],
+        out_specs=(in_vmem, in_vmem),
+        scratch_shapes=[pltpu.SemaphoreType.DMA((4,))],
+        name="pick",
+    )(keys, values)
+
+
+def keep_kernel(*refs):
+    pass
+
+
+def keep(far_kv, near_kv):
+    shape = pltpu.VMEM(far_kv.shape, BF16)
+    return pl.pallas_call(
+        keep_kernel,
+        out_shape=(shape, shape),
+        in_specs=[in_vmem, in_vmem],
+        out_specs=(in_vmem, in_vmem),
+        input_output_aliases={0: 0, 1: 1},
+        cost_estimate=pl.CostEstimate(flops=10**10, bytes_accessed=10**6, transcendentals=0),
+        compiler_params=pltpu.CompilerParams(vmem_limit_bytes=VMEM_LIMIT),
+        name="keep",
+    )(far_kv, near_kv)
+
+
+def diagonal_kernel(doc, kv, queries, out_grad, weights, dprobs, stats):
+    near = near_slot()
+    q, do = queries.at[near, 0], out_grad.at[near, 0]
+    kv_heads = kv.shape[2] // HD
+    bias = linked(doc, near)
+    mask = causal(kv.shape[1], CHUNK)
+    for j in range(kv_heads):
+        k = kv[0, :, pl.ds(j * HD, HD)]
+        v = kv[1, :, pl.ds(j * HD, HD)]
+        for h in range(0, GROUP, 2):
+            first = (j * GROUP + h) * HD
+            at = pl.ds(first, CHUNK)
+            logits = jnp.where(mask, dot_t(k, lanes(q, first, 2)) * LOG2_SCALE, masked_score)
+            top = jnp.max(logits, axis=0, keepdims=True)
+            e = jnp.exp2(logits - top)
+            dp = dot_t(v, lanes(do, first, 2))
+            weights[:, at] = e
+            dprobs[:, at] = dp
+            stats[0:1, at] = top
+            stats[1:2, at] = jnp.sum(e, axis=0, keepdims=True)
+            stats[2:3, at] = jnp.sum(e * dp, axis=0, keepdims=True)
+            stats[3:4, at] = jnp.full((1, CHUNK), bias, F32)
+
+
+def diagonal(block_doc, kv, queries, out_grad):
+    _, _, piece_len, width = queries.shape
+    return pl.pallas_call(
+        diagonal_kernel,
+        out_shape=(
+            pltpu.VMEM((piece_len, width), F32),
+            pltpu.VMEM((piece_len, width), F32),
+            pltpu.VMEM((8, width), F32),
+        ),
+        in_specs=[in_smem, in_vmem, in_vmem, in_vmem],
+        out_specs=(in_vmem,) * 3,
+        compiler_params=pltpu.CompilerParams(vmem_limit_bytes=VMEM_LIMIT),
+        name="diagonal",
+    )(block_doc, kv, queries, out_grad)
+
+
+def whole_kernel(doc, kv, kv_before, queries, out_grad, before, own, p, ds):
+    far = far_slot()
+    q, do = queries.at[far, 0], out_grad.at[far, 0]
+    kv_heads = kv.shape[2] // HD
+    piece_len = kv.shape[1]
+    bias = linked(doc, far)
+    mask = causal(piece_len, CHUNK)
+    for j in range(kv_heads):
+        head = pl.ds(j * HD, HD)
+        k = jnp.concatenate([kv_before[0, :, head], kv[0, :, head]], axis=0)
+        v = jnp.concatenate([kv_before[1, :, head], kv[1, :, head]], axis=0)
+        for h in range(0, GROUP, 2):
+            first = (j * GROUP + h) * HD
+            at = pl.ds(first, CHUNK)
+            logits = dot_t(k, lanes(q, first, 2)) * LOG2_SCALE
+            cross = logits[:piece_len]
+            here = jnp.where(mask, logits[piece_len:], masked_score)
+            top = jnp.maximum(
+                jnp.max(cross, axis=0, keepdims=True) + bias, jnp.max(here, axis=0, keepdims=True)
+            )
+            e = jnp.concatenate([jnp.exp2(cross - (top - bias)), jnp.exp2(here - top)], axis=0)
+            dp = dot_t(v, lanes(do, first, 2))
+            ratio = 1.0 / jnp.sum(e, axis=0, keepdims=True)
+            delta = jnp.sum(e * dp, axis=0, keepdims=True) * ratio
+            prob = e * ratio
+            p[:, at] = prob.astype(BF16)
+            ds[:, at] = (prob * (dp - delta)).astype(BF16)
+        cols = pl.ds(j * GROUP * HD, GROUP * HD)
+        dk = dot(ds[:, cols], lanes(q, j * GROUP * HD, GROUP)) * SCALE
+        dv = dot(p[:, cols], lanes(do, j * GROUP * HD, GROUP))
+        before[0, :, head] = dk[:piece_len].astype(BF16)
+        before[1, :, head] = dv[:piece_len].astype(BF16)
+        own[0, :, head] = dk[piece_len:]
+        own[1, :, head] = dv[piece_len:]
+
+
+def whole(block_doc, kv, kv_before, queries, out_grad):
+    _, piece_len, features = kv.shape
+    width = queries.shape[3]
+    return pl.pallas_call(
+        whole_kernel,
+        out_shape=(
+            pltpu.VMEM((2, piece_len, features), BF16),
+            pltpu.VMEM((2, piece_len, features), F32),
+            pltpu.VMEM((2 * piece_len, width), BF16),
+            pltpu.VMEM((2 * piece_len, width), BF16),
+        ),
+        in_specs=[in_smem] + [in_vmem] * 4,
+        out_specs=(in_vmem,) * 4,
+        compiler_params=pltpu.CompilerParams(vmem_limit_bytes=VMEM_LIMIT),
+        name="whole",
+    )(block_doc, kv, kv_before, queries, out_grad)
+
+
+def cross_kernel(kv_before, queries, out_grad, stats, before, p, ds, after):
+    near = near_slot()
+    q, do = queries.at[near, 0], out_grad.at[near, 0]
+    piece_len, features = kv_before.shape[1:]
+    for j in range(features // HD):
+        head = pl.ds(j * HD, HD)
+        k = kv_before[0, :, head]
+        v = kv_before[1, :, head]
+        for h in range(0, GROUP, 2):
+            first = (j * GROUP + h) * HD
+            at = pl.ds(first, CHUNK)
+            top_here, total_here, dot_here, bias = (stats[i : i + 1, at] for i in range(4))
+            logits = dot_t(k, lanes(q, first, 2)) * LOG2_SCALE
+            top = jnp.maximum(jnp.max(logits, axis=0, keepdims=True) + bias, top_here)
+            e = jnp.exp2(logits - (top - bias))
+            dp = dot_t(v, lanes(do, first, 2))
+            shrink = jnp.exp2(top_here - top)
+            ratio = 1.0 / (total_here * shrink + jnp.sum(e, axis=0, keepdims=True))
+            delta = (dot_here * shrink + jnp.sum(e * dp, axis=0, keepdims=True)) * ratio
+            prob = e * ratio
+            p[:, at] = prob.astype(BF16)
+            ds[:, at] = (prob * (dp - delta)).astype(BF16)
+            after[0:1, at] = shrink * ratio
+            after[1:2, at] = delta
+        cols = pl.ds(j * GROUP * HD, GROUP * HD)
+        dk = dot(ds[:, cols], lanes(q, j * GROUP * HD, GROUP)) * SCALE
+        dv = dot(p[:, cols], lanes(do, j * GROUP * HD, GROUP))
+        before[0, :, head] = dk.astype(BF16)
+        before[1, :, head] = dv.astype(BF16)
+
+
+def cross(kv_before, queries, out_grad, stats):
+    _, piece_len, features = kv_before.shape
+    width = queries.shape[3]
+    return pl.pallas_call(
+        cross_kernel,
+        out_shape=(
+            pltpu.VMEM((2, piece_len, features), BF16),
+            pltpu.VMEM((piece_len, width), BF16),
+            pltpu.VMEM((piece_len, width), BF16),
+            pltpu.VMEM((8, width), F32),
+        ),
+        in_specs=[in_vmem] * 4,
+        out_specs=(in_vmem,) * 4,
+        compiler_params=pltpu.CompilerParams(vmem_limit_bytes=VMEM_LIMIT),
+        name="cross",
+    )(kv_before, queries, out_grad, stats)
+
+
+def turn(wide, ref, first):
+    for i in range(wide.shape[1] // HD):
+        ref[:, pl.ds(first + i * HD, HD)] = wide[:, i * HD : (i + 1) * HD].T
+
+
+def rest_kernel(
+    near_kv, next_kv, queries, out_grad, weights, dprobs, p_next, ds_next, after, passed, far_kv, mate_kv,
+    p_far, ds_far, out, q_grad, k_grad, v_grad, o, dq, p, ds, dk_low, dv_low, sems,
+):
+    near, far = near_slot(), far_slot()
+    q, do = queries.at[near, 0], out_grad.at[near, 0]
+    kv_heads = near_kv.shape[2] // HD
+    span = GROUP * HD
+    backs = []
+
+    def give_back(side, slot, j):
+        cols = pl.ds(j * span, span)
+        for n, (a, b) in enumerate(((o, out), (dq, q_grad))):
+            sem = sems.at[2 + (side * kv_heads + j) * 2 + n]
+            back = pltpu.make_async_copy(a.at[side, :, cols], b.at[slot, 0, :, cols], sem)
+            back.start()
+            backs.append(back)
+
+    for j in range(kv_heads):
+        head = pl.ds(j * HD, HD)
+        k_t = jnp.concatenate([mate_kv[0, :, head], far_kv[0, :, head]], axis=0).T
+        v_t = jnp.concatenate([mate_kv[1, :, head], far_kv[1, :, head]], axis=0).T
+        for h in range(0, GROUP, 2):
+            first = (j * GROUP + h) * HD
+            at = pl.ds(first, CHUNK)
+            turn(dot(v_t, p_far[:, at]).astype(BF16), o.at[1], first)
+            turn((dot(k_t, ds_far[:, at]) * SCALE).astype(BF16), dq.at[1], first)
+        give_back(1, far, j)
+    for j in range(kv_heads):
+        head = pl.ds(j * HD, HD)
+        k_t = jnp.concatenate([next_kv[0, :, head], near_kv[0, :, head]], axis=0).T
+        v_t = jnp.concatenate([next_kv[1, :, head], near_kv[1, :, head]], axis=0).T
+        for h in range(0, GROUP, 2):
+            first = (j * GROUP + h) * HD
+            at = pl.ds(first, CHUNK)
+            prob = weights[:, at] * after[0:1, at]
+            prob_low = prob.astype(BF16)
+            ds_low = (prob * (dprobs[:, at] - after[1:2, at])).astype(BF16)
+            p[:, pl.ds(h * HD, CHUNK)] = prob_low
+            ds[:, pl.ds(h * HD, CHUNK)] = ds_low
+            turn(dot(v_t, jnp.concatenate([p_next[:, at], prob_low], axis=0)).astype(BF16), o.at[0], first)
+            dq_t = dot(k_t, jnp.concatenate([ds_next[:, at], ds_low], axis=0)) * SCALE
+            turn(dq_t.astype(BF16), dq.at[0], first)
+        give_back(0, near, j)
+        dk = dot(ds[...], lanes(q, j * span, GROUP)) * SCALE
+        dv = dot(p[...], lanes(do, j * span, GROUP))
+        dk_low[:, head] = (dk + passed[0, :, head].astype(F32)).astype(BF16)
+        dv_low[:, head] = (dv + passed[1, :, head].astype(F32)).astype(BF16)
+    backs += fetch_pairs([(dk_low, k_grad.at[near, 0]), (dv_low, v_grad.at[near, 0])], sems)
+    for back in backs:
+        back.wait()
+
+
+def rest(*operands, shape):
+    _, piece_len, features = operands[0].shape
+    width = shape[3]
+    kv_heads = features // HD
+    wide = jax.ShapeDtypeStruct(shape, BF16)
+    small = jax.ShapeDtypeStruct(shape[:3] + (features,), BF16)
+    return pl.pallas_call(
+        rest_kernel,
+        out_shape=(wide, wide, small, small),
+        in_specs=[in_vmem] * len(operands),
+        out_specs=(in_hbm,) * 4,
+        scratch_shapes=[pltpu.VMEM((2, piece_len, width), BF16)] * 2
+        + [pltpu.VMEM((piece_len, GROUP * HD), BF16)] * 2
+        + [pltpu.VMEM((piece_len, features), BF16)] * 2
+        + [pltpu.SemaphoreType.DMA((2 + 4 * kv_heads,))],
+        compiler_params=pltpu.CompilerParams(vmem_limit_bytes=VMEM_LIMIT),
+        name="rest",
+    )(*operands)
+
+
+def total_kernel(own, passed, k_grad_in, v_grad_in, k_grad, v_grad, low, sems):
+    far = far_slot()
+    low[...] = (own[...] + passed[...].astype(F32)).astype(BF16)
+    copies = fetch_pairs([(low.at[0], k_grad.at[far, 0]), (low.at[1], v_grad.at[far, 0])], sems)
+    for copy in copies:
+        copy.wait()
+
+
+def total(own, passed, k_grad, v_grad):
+    return pl.pallas_call(
+        total_kernel,
+        out_shape=(jax.ShapeDtypeStruct(k_grad.shape, BF16),) * 2,
+        in_specs=[in_vmem] * 2 + [in_hbm] * 2,
+        out_specs=(in_hbm,) * 2,
+        input_output_aliases={2: 0, 3: 1},
+        scratch_shapes=[pltpu.VMEM(own.shape, BF16), pltpu.SemaphoreType.DMA((2,))],
+        compiler_params=pltpu.CompilerParams(vmem_limit_bytes=VMEM_LIMIT),
+        name="total",
+    )(own, passed, k_grad, v_grad)
+
+
+def local_pairs(queries, keys, values, out_grad, block_doc):
+    pairs = lax.axis_size("ctx")
+    mates = [(i, i ^ 1) for i in range(pairs) if i ^ 1 < pairs]
+    low_route = [(i, i + 1) for i in range(3, pairs - 1, 2)]
+    high_route = [(i + 1, i) for i in range(1, pairs - 3, 2)]
+    route = low_route + high_route
+    route_back = [(b, a) for a, b in route]
+    far_kv, near_kv = keep(*pick(keys, values))
+    mate_kv = lax.ppermute(near_kv, "ctx", mates)
+    next_kv = lax.ppermute(far_kv, "ctx", route)
+    weights, dprobs, stats = diagonal(block_doc, near_kv, queries, out_grad)
+    mate_grads, own_grads, p_far, ds_far = whole(block_doc, far_kv, mate_kv, queries, out_grad)
+    mate_back = lax.ppermute(mate_grads, "ctx", mates)
+    next_grads, p_next, ds_next, after = cross(next_kv, queries, out_grad, stats)
+    next_back = lax.ppermute(next_grads, "ctx", route_back)
+    out, q_grad, k_grad, v_grad = rest(
+        near_kv, next_kv, queries, out_grad, weights, dprobs, p_next, ds_next, after, mate_back,
+        far_kv, mate_kv, p_far, ds_far, shape=queries.shape,
+    )
+    k_grad, v_grad = total(own_grads, next_back, k_grad, v_grad)
+    return (out, q_grad, k_grad, v_grad)
+
+
+def local(queries, keys, values, out_grad, block_doc):
+    window = min(7, lax.axis_size("ctx") // 4 - 1) + 1
+    piece_len = queries.shape[2]
+    if window == 2 and piece_len == BLOCK:
+        return local_pairs(queries, keys, values, out_grad, block_doc)
+    return local_wide(queries, keys, values, out_grad, block_doc)
+
+
 def solution(mesh):
     in_specs = (
         P(None, "ctx", None, "tp"),

time: 44.1 us -> 19.8 us (0.45)
  local copies, waits for them, and re-layouts: 9.55 us -> 0.02 us
  Pallas kernels: 0 us -> 8.88 us
  other arithmetic: 8.62 us -> 0 us
  matrix products: 7.67 us -> 0 us
  starting transfers between devices: 12.1 us -> 7.17 us
  between operations: 3.74 us -> 0.76 us
  waiting for transfers between devices: 1.95 us -> 2.72 us
    pallas_call x0 -> x7, Pallas kernels: none -> 8.88 us  [the longest x1 2.7 us: whole(): pl.pallas_call(whole_kernel, out_shape=(pltpu.VMEM((2, piece_len, feature...]
    dot_general x12 -> x0, matrix products: 7.67 us -> none  [the longest x4 3.18 us: per_key(): jnp.einsum(form, weights, right, preferred_element_type=jnp.float32)]
    ppermute x4, starting transfers between devices: 12.1 us -> 7.17 us  [the longest x1 3.21 us: local_pairs(): next_back = lax.ppermute(next_grads, 'ctx', route_back)]
    concatenate x4 -> x0, other arithmetic: 3.03 us -> none  [the longest x2 1.24 us: attend(): visible = jnp.concatenate(visible_rows, axis=1)]
    another operation x17 -> x0, local copies, waits for them, and re-layouts: 2.81 us -> none  [the longest x1 0.92 us: local(): paired = jnp.stack([keys[:, 0], values[:, 0]], axis=1)]
    unnamed x19 -> x6, local copies, waits for them, and re-layouts: 2.41 us -> 0.02 us
    broadcast_in_dim x2 -> x0, other arithmetic: 2.12 us -> none  [the longest x1 1.06 us: local(): qgrad_pair = jnp.stack([low_qgrad, high_qgrad])[:, None]]
    slice x7 -> x0, local copies, waits for them, and re-layouts: 1.53 us -> none  [the longest x1 1.36 us: local(): query_all[0]]
  transfers between devices with their start and end apart: 4 -> 4, of which waited for: 1 -> 2; matrix products, arithmetic and copies ran while one was open for 37% -> 0% of each run, Pallas kernels for 0% -> 37%
where the time goes in v1:
time: 19.8 us; the launch traced here: 19.6 us
  Pallas kernels  8.88 us (45%)
  starting transfers between devices  7.17 us (36%)
  waiting for transfers between devices  2.72 us (14%)
  between operations  0.76 us (4%)
    ppermute x1, starting transfers between devices, local_pairs(): next_back = lax.ppermute(next_grads, 'ctx', route_back)  3.21 us
    ppermute x1, starting transfers between devices, local_pairs(): next_kv = lax.ppermute(far_kv, 'ctx', route)  3.15 us
    pallas_call x1, Pallas kernels, whole(): pl.pallas_call(whole_kernel, out_shape=(pltpu.VMEM((2, piece_len, feature...  2.7 us
    pallas_call x1, Pallas kernels, rest(): pl.pallas_call(rest_kernel, out_shape=(wide, wide, small, small), in_spec...  2.19 us
    ppermute x1, waiting for transfers between devices, local_pairs(): next_back = lax.ppermute(next_grads, 'ctx', route_back)  1.76 us
    pallas_call x1, Pallas kernels, cross(): pl.pallas_call(cross_kernel, out_shape=(pltpu.VMEM((2, piece_len, feature...  1.16 us
    pallas_call x1, Pallas kernels, diagonal(): pl.pallas_call(diagonal_kernel, out_shape=(pltpu.VMEM((piece_len, width),...  1.16 us
    pallas_call x1, Pallas kernels, pick(): pl.pallas_call(pick_kernel, out_shape=(shape, shape), in_specs=[in_hbm, i...  0.98 us
  transfers between devices with their start and end apart: 4, of which 2 were waited for; matrix products, arithmetic and copies ran while one was open for 0% of the time, Pallas kernels for 37%

profile of v1, /device:TPU:27, one launch (start us, length us, event | category | flops | bytes accessed | tf_op | source)
XLA Modules:
  0.0 19.6 jit_solution(5192787458648271832)
XLA Ops:
  0.6 1.0 %pick.1 = (bf16[2,128,256]{2,1,0:T(8,128)(2,1)S(1)}, bf16[2,128,256]{2,1,0:T(8,128)(2,1)S(1)}) custom-call(bf16[2,1,128,256]{3,2,1,0:T(8,128)(2,1)} %keys.1, bf16[2,1,128,256]{3,2,1,0:T(8,128)(2,1)} %values.1), custom_call_target="tpu_custom_call" | custom-call | tf_op jit(solution)/shard_map/pick/pallas_call | solution.py:212
  1.6 0.0 copy-start
  1.6 0.0 copy-start.1
  1.7 0.0 copy-start.2
  1.7 0.7 %collective-permute-start.1 = (bf16[2,128,256]{2,1,0:T(8,128)(2,1)S(1)}, bf16[2,128,256]{2,1,0:T(8,128)(2,1)S(1)}, u32[]{:S(2)}, u32[]{:S(2)}) collective-permute-start(bf16[2,128,256]{2,1,0:T(8,128)(2,1)S(1)} %get-tuple-element.27.kv.near_kv), channel_id=1, source_target_pairs={{0,4},{4,0},{8,12},{12,8},{16,20},{20,16},{24,28},{28,24},{1,5},{5... | collective-permute-start | bytes 393224 | tf_op jit(solution)/shard_map/ppermute | solution.py:490
  2.4 3.1 %collective-permute-start = (bf16[2,128,256]{2,1,0:T(8,128)(2,1)S(1)}, bf16[2,128,256]{2,1,0:T(8,128)(2,1)S(1)}, u32[]{:S(2)}, u32[]{:S(2)}) collective-permute-start(bf16[2,128,256]{2,1,0:T(8,128)(2,1)S(1)} %get-tuple-element.28.kv.far_kv), channel_id=1, source_target_pairs={{12,16},{20,24},{8,4},{16,12},{13,17},{21,25},{9,5},{17,13},{14,18... | collective-permute-start | bytes 393224 | tf_op jit(solution)/shard_map/ppermute | solution.py:491
  5.6 0.0 collective-permute-done.1.kv_before.mate_kv
  5.6 0.0 copy-done
  5.6 0.0 copy-done.1
  5.6 0.0 copy-done.2
  5.6 2.7 %whole.1 = (bf16[2,128,256]{2,1,0:T(8,128)(2,1)S(1)}, f32[2,128,256]{2,1,0:T(8,128)S(1)}, bf16[256,2048]{1,0:T(8,128)(2,1)S(1)}, bf16[256,2048]{1,0:T(8,128)(2,1)S(1)}) custom-call(s32[16]{0:T(128)S(1)} %copy-done.2, bf16[2,128,256]{2,1,0:T(8,128)(2,1)S(1)} %get-tuple-element.28.kv.far_kv, bf16[2,128,256]{2,1,0:T(8,128)(2,1)S(1)} %collective-permute-done.1.kv_before.mate_kv, ...), custom_call_target="tpu_custom_call" | custom-call | tf_op jit(solution)/shard_map/whole/pallas_call | solution.py:319
  8.3 0.1 collective-permute-start.2
  8.4 1.2 %diagonal.1 = (f32[128,2048]{1,0:T(8,128)S(1)}, f32[128,2048]{1,0:T(8,128)S(1)}, f32[8,2048]{1,0:T(8,128)S(1)}) custom-call(s32[16]{0:T(128)S(1)} %copy-done.2, bf16[2,128,256]{2,1,0:T(8,128)(2,1)S(1)} %get-tuple-element.27.kv.near_kv, bf16[2,1,128,2048]{3,2,1,0:T(8,128)(2,1)S(1)} %copy-done, bf16[2,1,128,2048]{3,2,1,0:T(8,128)(2,1)S(1)} %copy-done.1), custom_call_target="tpu_custom_call" | custom-call | tf_op jit(solution)/shard_map/diagonal/pallas_call | solution.py:266
  9.5 1.0 %collective-permute-done.kv_before.next_kv = bf16[2,128,256]{2,1,0:T(8,128)(2,1)S(1)} collective-permute-done((bf16[2,128,256]{2,1,0:T(8,128)(2,1)S(1)}, bf16[2,128,256]{2,1,0:T(8,128)(2,1)S(1)}, u32[]{:S(2)}, u32[]{:S(2)}) %collective-permute-start) | collective-permute-done | bytes 131104 | tf_op jit(solution)/shard_map/ppermute | solution.py:491
  10.5 1.2 %cross.1 = (bf16[2,128,256]{2,1,0:T(8,128)(2,1)S(1)}, bf16[128,2048]{1,0:T(8,128)(2,1)S(1)}, bf16[128,2048]{1,0:T(8,128)(2,1)S(1)}, f32[8,2048]{1,0:T(8,128)S(1)}) custom-call(bf16[2,128,256]{2,1,0:T(8,128)(2,1)S(1)} %collective-permute-done.kv_before.next_kv, bf16[2,1,128,2048]{3,2,1,0:T(8,128)(2,1)S(1)} %copy-done, ...), custom_call_target="tpu_custom_call" | custom-call | tf_op jit(solution)/shard_map/cross/pallas_call | solution.py:368
  11.7 3.2 %collective-permute-start.3 = (bf16[2,128,256]{2,1,0:T(8,128)(2,1)S(1)}, bf16[2,128,256]{2,1,0:T(8,128)(2,1)S(1)}, u32[]{:S(2)}, u32[]{:S(2)}) collective-permute-start(bf16[2,128,256]{2,1,0:T(8,128)(2,1)S(1)} %get-tuple-element.41), channel_id=1, source_target_pairs={{16,12},{24,20},{4,8},{12,16},{17,13},{25,21},{5,9},{13,17},{18,14... | collective-permute-start | bytes 393224 | tf_op jit(solution)/shard_map/ppermute | solution.py:496
  14.9 0.0 collective-permute-done.2.passed
  14.9 2.2 %rest.1 = (bf16[2,1,128,2048]{3,2,1,0:T(8,128)(2,1)}, bf16[2,1,128,2048]{3,2,1,0:T(8,128)(2,1)}, bf16[2,1,128,256]{3,2,1,0:T(8,128)(2,1)}, bf16[2,1,128,256]{3,2,1,0:T(8,128)(2,1)}) custom-call(bf16[2,128,256]{2,1,0:T(8,128)(2,1)S(1)} %get-tuple-element.27.kv.near_kv, bf16[2,128,256]{2,1,0:T(8,128)(2,1)S(1)} %collective-permute-done.kv_before.next_kv, ...), custom_call_target="tpu_custom_call" | custom-call | tf_op jit(solution)/shard_map/rest/pallas_call | solution.py:447
  17.1 1.8 %collective-permute-done.3.passed = bf16[2,128,256]{2,1,0:T(8,128)(2,1)S(1)} collective-permute-done((bf16[2,128,256]{2,1,0:T(8,128)(2,1)S(1)}, bf16[2,128,256]{2,1,0:T(8,128)(2,1)S(1)}, u32[]{:S(2)}, u32[]{:S(2)}) %collective-permute-start.3) | collective-permute-done | bytes 131104 | tf_op jit(solution)/shard_map/ppermute | solution.py:496
  18.9 0.7 %total.1 = (bf16[2,1,128,256]{3,2,1,0:T(8,128)(2,1)}, bf16[2,1,128,256]{3,2,1,0:T(8,128)(2,1)}) custom-call(f32[2,128,256]{2,1,0:T(8,128)S(1)} %get-tuple-element.40.own, bf16[2,128,256]{2,1,0:T(8,128)(2,1)S(1)} %collective-permute-done.3.passed, bf16[2,1,128,256]{3,2,1,0:T(8,128)(2,1)} %get-tuple-element.42.k_grad_in, ...), custom_call_target="tpu_custom_call", output_to_operand_aliasing={{0}: (2, {}), {1}: (3, {})} | custom-call | tf_op jit(solution)/shard_map/total/pallas_call | solution.py:470
  (1 shorter events, 0.0 us)
Async XLA Ops:
  1.6 4.0 %copy-start = (bf16[2,1,128,2048]{3,2,1,0:T(8,128)(2,1)S(1)}, bf16[2,1,128,2048]{3,2,1,0:T(8,128)(2,1)}, u32[]{:S(2)}) copy-start(bf16[2,1,128,2048]{3,2,1,0:T(8,128)(2,1)} %queries.7) | copy-start | bytes 3145732
  1.6 4.0 %copy-start.1 = (bf16[2,1,128,2048]{3,2,1,0:T(8,128)(2,1)S(1)}, bf16[2,1,128,2048]{3,2,1,0:T(8,128)(2,1)}, u32[]{:S(2)}) copy-start(bf16[2,1,128,2048]{3,2,1,0:T(8,128)(2,1)} %out_grad.7) | copy-start | bytes 3145732
  1.7 3.9 %copy-start.2 = (s32[16]{0:T(128)S(1)}, s32[16]{0:T(128)}, u32[]{:S(2)}) copy-start(s32[16]{0:T(128)} %doc.3) | copy-start | bytes 196
  1.7 3.9 %collective-permute-start.1 = (bf16[2,128,256]{2,1,0:T(8,128)(2,1)S(1)}, bf16[2,128,256]{2,1,0:T(8,128)(2,1)S(1)}, u32[]{:S(2)}, u32[]{:S(2)}) collective-permute-start(bf16[2,128,256]{2,1,0:T(8,128)(2,1)S(1)} %get-tuple-element.27.kv.near_kv), channel_id=1, source_target_pairs={{0,4},{4,0},{8,12},{12,8},{16,20},{20,16},{24,28},{28,24},{1,5},{5... | collective-permute-start | bytes 393224 | tf_op jit(solution)/shard_map/ppermute | solution.py:490
  2.4 8.1 %collective-permute-start = (bf16[2,128,256]{2,1,0:T(8,128)(2,1)S(1)}, bf16[2,128,256]{2,1,0:T(8,128)(2,1)S(1)}, u32[]{:S(2)}, u32[]{:S(2)}) collective-permute-start(bf16[2,128,256]{2,1,0:T(8,128)(2,1)S(1)} %get-tuple-element.28.kv.far_kv), channel_id=1, source_target_pairs={{12,16},{20,24},{8,4},{16,12},{13,17},{21,25},{9,5},{17,13},{14,18... | collective-permute-start | bytes 393224 | tf_op jit(solution)/shard_map/ppermute | solution.py:491
  8.3 6.6 %collective-permute-start.2 = (bf16[2,128,256]{2,1,0:T(8,128)(2,1)S(1)}, bf16[2,128,256]{2,1,0:T(8,128)(2,1)S(1)}, u32[]{:S(2)}, u32[]{:S(2)}) collective-permute-start(bf16[2,128,256]{2,1,0:T(8,128)(2,1)S(1)} %get-tuple-element.35), channel_id=1, source_target_pairs={{0,4},{4,0},{8,12},{12,8},{16,20},{20,16},{24,28},{28,24},{1,5},{5... | collective-permute-start | bytes 393224 | tf_op jit(solution)/shard_map/ppermute | solution.py:494
  11.7 7.2 %collective-permute-start.3 = (bf16[2,128,256]{2,1,0:T(8,128)(2,1)S(1)}, bf16[2,128,256]{2,1,0:T(8,128)(2,1)S(1)}, u32[]{:S(2)}, u32[]{:S(2)}) collective-permute-start(bf16[2,128,256]{2,1,0:T(8,128)(2,1)S(1)} %get-tuple-element.41), channel_id=1, source_target_pairs={{16,12},{24,20},{4,8},{12,16},{17,13},{25,21},{5,9},{13,17},{18,14... | collective-permute-start | bytes 393224 | tf_op jit(solution)/shard_map/ppermute | solution.py:496

commit v2 on v1

--- a/solution.py
+++ b/solution.py
@@ -242,6 +242,7 @@
     q, do = queries.at[near, 0], out_grad.at[near, 0]
     kv_heads = kv.shape[2] // HD
     bias = linked(doc, near)
+    bias_far = linked(doc, 1 - near)
     mask = causal(kv.shape[1], CHUNK)
     for j in range(kv_heads):
         k = kv[0, :, pl.ds(j * HD, HD)]
@@ -259,6 +260,7 @@
             stats[1:2, at] = jnp.sum(e, axis=0, keepdims=True)
             stats[2:3, at] = jnp.sum(e * dp, axis=0, keepdims=True)
             stats[3:4, at] = jnp.full((1, CHUNK), bias, F32)
+            stats[4:5, at] = jnp.full((1, CHUNK), bias_far, F32)
 
 
 def diagonal(block_doc, kv, queries, out_grad):
@@ -277,12 +279,12 @@
     )(block_doc, kv, queries, out_grad)
 
 
-def whole_kernel(doc, kv, kv_before, queries, out_grad, before, own, p, ds):
+def whole_kernel(stats, kv, kv_before, queries, out_grad, before, own, p, ds):
     far = far_slot()
     q, do = queries.at[far, 0], out_grad.at[far, 0]
     kv_heads = kv.shape[2] // HD
     piece_len = kv.shape[1]
-    bias = linked(doc, far)
+    bias = stats[4:5, :CHUNK]
     mask = causal(piece_len, CHUNK)
     for j in range(kv_heads):
         head = pl.ds(j * HD, HD)
@@ -313,7 +315,7 @@
         own[1, :, head] = dv[piece_len:]
 
 
-def whole(block_doc, kv, kv_before, queries, out_grad):
+def whole(stats, kv, kv_before, queries, out_grad):
     _, piece_len, features = kv.shape
     width = queries.shape[3]
     return pl.pallas_call(
@@ -324,11 +326,11 @@
             pltpu.VMEM((2 * piece_len, width), BF16),
             pltpu.VMEM((2 * piece_len, width), BF16),
         ),
-        in_specs=[in_smem] + [in_vmem] * 4,
+        in_specs=[in_vmem] * 5,
         out_specs=(in_vmem,) * 4,
         compiler_params=pltpu.CompilerParams(vmem_limit_bytes=VMEM_LIMIT),
         name="whole",
-    )(block_doc, kv, kv_before, queries, out_grad)
+    )(stats, kv, kv_before, queries, out_grad)
 
 
 def cross_kernel(kv_before, queries, out_grad, stats, before, p, ds, after):
@@ -479,18 +481,34 @@
     )(own, passed, k_grad, v_grad)
 
 
+def complete(route, pairs, flip=False):
+    sources = [i for i in range(pairs) if i not in {a for a, _ in route}]
+    targets = [i for i in range(pairs) if i not in {b for _, b in route}]
+    spare = [(i, i ^ 1) for i in sources if i ^ 1 in targets]
+    sources = [i for i in sources if i not in {a for a, _ in spare}]
+    targets = [i for i in targets if i not in {b for _, b in spare}]
+    if flip:
+        targets = targets[::-1]
+    for turn_by in range(max(1, len(targets))):
+        turned = targets[turn_by:] + targets[:turn_by]
+        if all(a != b for a, b in zip(sources, turned)):
+            return route + spare + list(zip(sources, turned))
+    return route
+
+
 def local_pairs(queries, keys, values, out_grad, block_doc):
     pairs = lax.axis_size("ctx")
     mates = [(i, i ^ 1) for i in range(pairs) if i ^ 1 < pairs]
     low_route = [(i, i + 1) for i in range(3, pairs - 1, 2)]
     high_route = [(i + 1, i) for i in range(1, pairs - 3, 2)]
-    route = low_route + high_route
-    route_back = [(b, a) for a, b in route]
+    links = low_route + high_route
+    route = complete(links, pairs)
+    route_back = complete([(b, a) for a, b in links], pairs, flip=True)
     far_kv, near_kv = keep(*pick(keys, values))
     mate_kv = lax.ppermute(near_kv, "ctx", mates)
     next_kv = lax.ppermute(far_kv, "ctx", route)
     weights, dprobs, stats = diagonal(block_doc, near_kv, queries, out_grad)
-    mate_grads, own_grads, p_far, ds_far = whole(block_doc, far_kv, mate_kv, queries, out_grad)
+    mate_grads, own_grads, p_far, ds_far = whole(stats, far_kv, mate_kv, queries, out_grad)
     mate_back = lax.ppermute(mate_grads, "ctx", mates)
     next_grads, p_next, ds_next, after = cross(next_kv, queries, out_grad, stats)
     next_back = lax.ppermute(next_grads, "ctx", route_back)

time: 19.8 us -> 15.9 us (0.80)
  starting transfers between devices: 7.17 us -> 3.67 us
  Pallas kernels: 8.88 us -> 8.34 us
  waiting for transfers between devices: 2.72 us -> 3.02 us
    ppermute x1, starting transfers between devices: 3.15 us -> 1.17 us  [local_pairs(): next_kv = lax.ppermute(far_kv, 'ctx', route)]
    ppermute x1, starting transfers between devices: 3.21 us -> 1.44 us  [local_pairs(): next_back = lax.ppermute(next_grads, 'ctx', route_back)]
    pallas_call x1, Pallas kernels: 2.7 us -> 2.15 us  [whole(): pl.pallas_call(whole_kernel, out_shape=(pltpu.VMEM((2, piece_len, feature...]
    ppermute x1, waiting for transfers between devices: 0.96 us -> 1.31 us  [local_pairs(): next_kv = lax.ppermute(far_kv, 'ctx', route)]
    ppermute x1, starting transfers between devices: 0.07 us -> 0.33 us  [local_pairs(): mate_back = lax.ppermute(mate_grads, 'ctx', mates)]
  transfers between devices with their start and end apart: 4 -> 4, of which waited for: 2 -> 2; matrix products, arithmetic and copies ran while one was open for 0% -> 0% of each run, Pallas kernels for 37% -> 42%
where the time goes in v2:
time: 15.9 us; the launch traced here: 15.8 us
  Pallas kernels  8.34 us (52%)
  starting transfers between devices  3.67 us (23%)
  waiting for transfers between devices  3.02 us (19%)
  between operations  0.71 us (4%)
    pallas_call x1, Pallas kernels, rest(): pl.pallas_call(rest_kernel, out_shape=(wide, wide, small, small), in_spec...  2.19 us
    pallas_call x1, Pallas kernels, whole(): pl.pallas_call(whole_kernel, out_shape=(pltpu.VMEM((2, piece_len, feature...  2.15 us
    ppermute x1, waiting for transfers between devices, local_pairs(): next_back = lax.ppermute(next_grads, 'ctx', route_back)  1.71 us
    ppermute x1, starting transfers between devices, local_pairs(): next_back = lax.ppermute(next_grads, 'ctx', route_back)  1.44 us
    ppermute x1, waiting for transfers between devices, local_pairs(): next_kv = lax.ppermute(far_kv, 'ctx', route)  1.31 us
    ppermute x1, starting transfers between devices, local_pairs(): next_kv = lax.ppermute(far_kv, 'ctx', route)  1.17 us
    pallas_call x1, Pallas kernels, cross(): pl.pallas_call(cross_kernel, out_shape=(pltpu.VMEM((2, piece_len, feature...  1.17 us
    pallas_call x1, Pallas kernels, diagonal(): pl.pallas_call(diagonal_kernel, out_shape=(pltpu.VMEM((piece_len, width),...  1.15 us
  transfers between devices with their start and end apart: 4, of which 2 were waited for; matrix products, arithmetic and copies ran while one was open for 0% of the time, Pallas kernels for 42%

profile of v2, /device:TPU:27, one launch (start us, length us, event | category | flops | bytes accessed | tf_op | source)
XLA Modules:
  0.0 15.8 jit_solution(6856186811776530403)
XLA Ops:
  0.6 1.0 %pick.1 = (bf16[2,128,256]{2,1,0:T(8,128)(2,1)S(1)}, bf16[2,128,256]{2,1,0:T(8,128)(2,1)S(1)}) custom-call(bf16[2,1,128,256]{3,2,1,0:T(8,128)(2,1)} %keys.1, bf16[2,1,128,256]{3,2,1,0:T(8,128)(2,1)} %values.1), custom_call_target="tpu_custom_call" | custom-call | tf_op jit(solution)/shard_map/pick/pallas_call | solution.py:212
  1.6 0.0 copy-start
  1.6 0.0 copy-start.1
  1.7 0.0 copy-start.2
  1.7 0.7 %collective-permute-start.1 = (bf16[2,128,256]{2,1,0:T(8,128)(2,1)S(1)}, bf16[2,128,256]{2,1,0:T(8,128)(2,1)S(1)}, u32[]{:S(2)}, u32[]{:S(2)}) collective-permute-start(bf16[2,128,256]{2,1,0:T(8,128)(2,1)S(1)} %get-tuple-element.27.kv.near_kv), channel_id=1, source_target_pairs={{0,4},{4,0},{8,12},{12,8},{16,20},{20,16},{24,28},{28,24},{1,5},{5... | collective-permute-start | bytes 393224 | tf_op jit(solution)/shard_map/ppermute | solution.py:508
  2.4 1.2 %collective-permute-start = (bf16[2,128,256]{2,1,0:T(8,128)(2,1)S(1)}, bf16[2,128,256]{2,1,0:T(8,128)(2,1)S(1)}, u32[]{:S(2)}, u32[]{:S(2)}) collective-permute-start(bf16[2,128,256]{2,1,0:T(8,128)(2,1)S(1)} %get-tuple-element.28.kv.far_kv), channel_id=1, source_target_pairs={{12,16},{20,24},{8,4},{16,12},{4,0},{24,28},{0,8},{28,20},{13,17},... | collective-permute-start | bytes 393224 | tf_op jit(solution)/shard_map/ppermute | solution.py:509
  3.6 0.0 copy-done
  3.6 0.0 copy-done.1
  3.6 0.0 copy-done.2
  3.6 1.2 %diagonal.1 = (f32[128,2048]{1,0:T(8,128)S(1)}, f32[128,2048]{1,0:T(8,128)S(1)}, f32[8,2048]{1,0:T(8,128)S(1)}) custom-call(s32[16]{0:T(128)S(1)} %copy-done.2, bf16[2,128,256]{2,1,0:T(8,128)(2,1)S(1)} %get-tuple-element.27.kv.near_kv, bf16[2,1,128,2048]{3,2,1,0:T(8,128)(2,1)S(1)} %copy-done, bf16[2,1,128,2048]{3,2,1,0:T(8,128)(2,1)S(1)} %copy-done.1), custom_call_target="tpu_custom_call" | custom-call | tf_op jit(solution)/shard_map/diagonal/pallas_call | solution.py:268
  4.7 0.0 collective-permute-done.1.kv_before.mate_kv
  4.8 2.2 %whole.1 = (bf16[2,128,256]{2,1,0:T(8,128)(2,1)S(1)}, f32[2,128,256]{2,1,0:T(8,128)S(1)}, bf16[256,2048]{1,0:T(8,128)(2,1)S(1)}, bf16[256,2048]{1,0:T(8,128)(2,1)S(1)}) custom-call(f32[8,2048]{1,0:T(8,128)S(1)} %get-tuple-element.31.stats, bf16[2,128,256]{2,1,0:T(8,128)(2,1)S(1)} %get-tuple-element.28.kv.far_kv, ...), custom_call_target="tpu_custom_call" | custom-call | tf_op jit(solution)/shard_map/whole/pallas_call | solution.py:321
  6.9 0.3 %collective-permute-start.2 = (bf16[2,128,256]{2,1,0:T(8,128)(2,1)S(1)}, bf16[2,128,256]{2,1,0:T(8,128)(2,1)S(1)}, u32[]{:S(2)}, u32[]{:S(2)}) collective-permute-start(bf16[2,128,256]{2,1,0:T(8,128)(2,1)S(1)} %get-tuple-element.35), channel_id=1, source_target_pairs={{0,4},{4,0},{8,12},{12,8},{16,20},{20,16},{24,28},{28,24},{1,5},{5... | collective-permute-start | bytes 393224 | tf_op jit(solution)/shard_map/ppermute | solution.py:512
  7.2 1.3 %collective-permute-done.kv_before.next_kv = bf16[2,128,256]{2,1,0:T(8,128)(2,1)S(1)} collective-permute-done((bf16[2,128,256]{2,1,0:T(8,128)(2,1)S(1)}, bf16[2,128,256]{2,1,0:T(8,128)(2,1)S(1)}, u32[]{:S(2)}, u32[]{:S(2)}) %collective-permute-start) | collective-permute-done | bytes 131104 | tf_op jit(solution)/shard_map/ppermute | solution.py:509
  8.5 1.2 %cross.1 = (bf16[2,128,256]{2,1,0:T(8,128)(2,1)S(1)}, bf16[128,2048]{1,0:T(8,128)(2,1)S(1)}, bf16[128,2048]{1,0:T(8,128)(2,1)S(1)}, f32[8,2048]{1,0:T(8,128)S(1)}) custom-call(bf16[2,128,256]{2,1,0:T(8,128)(2,1)S(1)} %collective-permute-done.kv_before.next_kv, bf16[2,1,128,2048]{3,2,1,0:T(8,128)(2,1)S(1)} %copy-done, ...), custom_call_target="tpu_custom_call" | custom-call | tf_op jit(solution)/shard_map/cross/pallas_call | solution.py:370
  9.7 1.4 %collective-permute-start.3 = (bf16[2,128,256]{2,1,0:T(8,128)(2,1)S(1)}, bf16[2,128,256]{2,1,0:T(8,128)(2,1)S(1)}, u32[]{:S(2)}, u32[]{:S(2)}) collective-permute-start(bf16[2,128,256]{2,1,0:T(8,128)(2,1)S(1)} %get-tuple-element.41), channel_id=1, source_target_pairs={{16,12},{24,20},{4,8},{12,16},{0,4},{28,24},{8,28},{20,0},{17,13},... | collective-permute-start | bytes 393224 | tf_op jit(solution)/shard_map/ppermute | solution.py:514
  11.2 0.0 collective-permute-done.2.passed
  11.2 2.2 %rest.1 = (bf16[2,1,128,2048]{3,2,1,0:T(8,128)(2,1)}, bf16[2,1,128,2048]{3,2,1,0:T(8,128)(2,1)}, bf16[2,1,128,256]{3,2,1,0:T(8,128)(2,1)}, bf16[2,1,128,256]{3,2,1,0:T(8,128)(2,1)}) custom-call(bf16[2,128,256]{2,1,0:T(8,128)(2,1)S(1)} %get-tuple-element.27.kv.near_kv, bf16[2,128,256]{2,1,0:T(8,128)(2,1)S(1)} %collective-permute-done.kv_before.next_kv, ...), custom_call_target="tpu_custom_call" | custom-call | tf_op jit(solution)/shard_map/rest/pallas_call | solution.py:449
  13.4 1.7 %collective-permute-done.3.passed = bf16[2,128,256]{2,1,0:T(8,128)(2,1)S(1)} collective-permute-done((bf16[2,128,256]{2,1,0:T(8,128)(2,1)S(1)}, bf16[2,128,256]{2,1,0:T(8,128)(2,1)S(1)}, u32[]{:S(2)}, u32[]{:S(2)}) %collective-permute-start.3) | collective-permute-done | bytes 131104 | tf_op jit(solution)/shard_map/ppermute | solution.py:514
  15.1 0.7 %total.1 = (bf16[2,1,128,256]{3,2,1,0:T(8,128)(2,1)}, bf16[2,1,128,256]{3,2,1,0:T(8,128)(2,1)}) custom-call(f32[2,128,256]{2,1,0:T(8,128)S(1)} %get-tuple-element.40.own, bf16[2,128,256]{2,1,0:T(8,128)(2,1)S(1)} %collective-permute-done.3.passed, bf16[2,1,128,256]{3,2,1,0:T(8,128)(2,1)} %get-tuple-element.42.k_grad_in, ...), custom_call_target="tpu_custom_call", output_to_operand_aliasing={{0}: (2, {}), {1}: (3, {})} | custom-call | tf_op jit(solution)/shard_map/total/pallas_call | solution.py:472
  (1 shorter events, 0.0 us)
Async XLA Ops:
  1.6 2.0 %copy-start = (bf16[2,1,128,2048]{3,2,1,0:T(8,128)(2,1)S(1)}, bf16[2,1,128,2048]{3,2,1,0:T(8,128)(2,1)}, u32[]{:S(2)}) copy-start(bf16[2,1,128,2048]{3,2,1,0:T(8,128)(2,1)} %queries.7) | copy-start | bytes 3145732
  1.6 1.9 %copy-start.1 = (bf16[2,1,128,2048]{3,2,1,0:T(8,128)(2,1)S(1)}, bf16[2,1,128,2048]{3,2,1,0:T(8,128)(2,1)}, u32[]{:S(2)}) copy-start(bf16[2,1,128,2048]{3,2,1,0:T(8,128)(2,1)} %out_grad.7) | copy-start | bytes 3145732
  1.7 1.9 %copy-start.2 = (s32[16]{0:T(128)S(1)}, s32[16]{0:T(128)}, u32[]{:S(2)}) copy-start(s32[16]{0:T(128)} %doc.1) | copy-start | bytes 196
  1.7 3.1 %collective-permute-start.1 = (bf16[2,128,256]{2,1,0:T(8,128)(2,1)S(1)}, bf16[2,128,256]{2,1,0:T(8,128)(2,1)S(1)}, u32[]{:S(2)}, u32[]{:S(2)}) collective-permute-start(bf16[2,128,256]{2,1,0:T(8,128)(2,1)S(1)} %get-tuple-element.27.kv.near_kv), channel_id=1, source_target_pairs={{0,4},{4,0},{8,12},{12,8},{16,20},{20,16},{24,28},{28,24},{1,5},{5... | collective-permute-start | bytes 393224 | tf_op jit(solution)/shard_map/ppermute | solution.py:508
  2.4 6.1 %collective-permute-start = (bf16[2,128,256]{2,1,0:T(8,128)(2,1)S(1)}, bf16[2,128,256]{2,1,0:T(8,128)(2,1)S(1)}, u32[]{:S(2)}, u32[]{:S(2)}) collective-permute-start(bf16[2,128,256]{2,1,0:T(8,128)(2,1)S(1)} %get-tuple-element.28.kv.far_kv), channel_id=1, source_target_pairs={{12,16},{20,24},{8,4},{16,12},{4,0},{24,28},{0,8},{28,20},{13,17},... | collective-permute-start | bytes 393224 | tf_op jit(solution)/shard_map/ppermute | solution.py:509
  6.9 4.2 %collective-permute-start.2 = (bf16[2,128,256]{2,1,0:T(8,128)(2,1)S(1)}, bf16[2,128,256]{2,1,0:T(8,128)(2,1)S(1)}, u32[]{:S(2)}, u32[]{:S(2)}) collective-permute-start(bf16[2,128,256]{2,1,0:T(8,128)(2,1)S(1)} %get-tuple-element.35), channel_id=1, source_target_pairs={{0,4},{4,0},{8,12},{12,8},{16,20},{20,16},{24,28},{28,24},{1,5},{5... | collective-permute-start | bytes 393224 | tf_op jit(solution)/shard_map/ppermute | solution.py:512
  9.7 5.3 %collective-permute-start.3 = (bf16[2,128,256]{2,1,0:T(8,128)(2,1)S(1)}, bf16[2,128,256]{2,1,0:T(8,128)(2,1)S(1)}, u32[]{:S(2)}, u32[]{:S(2)}) collective-permute-start(bf16[2,128,256]{2,1,0:T(8,128)(2,1)S(1)} %get-tuple-element.41), channel_id=1, source_target_pairs={{16,12},{24,20},{4,8},{12,16},{0,4},{28,24},{8,28},{20,0},{17,13},... | collective-permute-start | bytes 393224 | tf_op jit(solution)/shard_map/ppermute | solution.py:514

commit v3 on v2

--- a/solution.py
+++ b/solution.py
@@ -1,3 +1,4 @@
+import functools
 import math
 
 import jax
@@ -191,10 +192,11 @@
     return copies
 
 
-def pick_kernel(keys, values, far_kv, near_kv, sems):
+def pick_kernel(needed, keys, values, block_doc, far_kv, near_kv, case, doc, sems):
     far, near = far_slot(), near_slot()
     copies = fetch_pairs(
         [
+            (block_doc, doc),
             (keys.at[far, 0], far_kv.at[0]),
             (values.at[far, 0], far_kv.at[1]),
             (keys.at[near, 0], near_kv.at[0]),
@@ -202,21 +204,28 @@
         ],
         sems,
     )
-    for copy in copies:
+    copies[0].wait()
+    case[0] = needed(doc)
+    for copy in copies[1:]:
         copy.wait()
 
 
-def pick(keys, values):
+def pick(keys, values, block_doc, needed):
     _, _, piece_len, features = keys.shape
     shape = pltpu.VMEM((2, piece_len, features), BF16)
     return pl.pallas_call(
-        pick_kernel,
-        out_shape=(shape, shape),
-        in_specs=[in_hbm, in_hbm],
-        out_specs=(in_vmem, in_vmem),
-        scratch_shapes=[pltpu.SemaphoreType.DMA((4,))],
+        functools.partial(pick_kernel, needed),
+        out_shape=(
+            shape,
+            shape,
+            pltpu.SMEM((1,), jnp.int32),
+            pltpu.SMEM(block_doc.shape, jnp.int32),
+        ),
+        in_specs=[in_hbm, in_hbm, in_hbm],
+        out_specs=(in_vmem, in_vmem, in_smem, in_smem),
+        scratch_shapes=[pltpu.SemaphoreType.DMA((5,))],
         name="pick",
-    )(keys, values)
+    )(keys, values, block_doc)
 
 
 def keep_kernel(*refs):
@@ -333,38 +342,51 @@
     )(stats, kv, kv_before, queries, out_grad)
 
 
-def cross_kernel(kv_before, queries, out_grad, stats, before, p, ds, after):
+def cross_kernel(kv_before, queries, out_grad, stats, behind, before, p, ds, after):
     near = near_slot()
     q, do = queries.at[near, 0], out_grad.at[near, 0]
     piece_len, features = kv_before.shape[1:]
-    for j in range(features // HD):
-        head = pl.ds(j * HD, HD)
-        k = kv_before[0, :, head]
-        v = kv_before[1, :, head]
-        for h in range(0, GROUP, 2):
-            first = (j * GROUP + h) * HD
-            at = pl.ds(first, CHUNK)
-            top_here, total_here, dot_here, bias = (stats[i : i + 1, at] for i in range(4))
-            logits = dot_t(k, lanes(q, first, 2)) * LOG2_SCALE
-            top = jnp.maximum(jnp.max(logits, axis=0, keepdims=True) + bias, top_here)
-            e = jnp.exp2(logits - (top - bias))
-            dp = dot_t(v, lanes(do, first, 2))
-            shrink = jnp.exp2(top_here - top)
-            ratio = 1.0 / (total_here * shrink + jnp.sum(e, axis=0, keepdims=True))
-            delta = (dot_here * shrink + jnp.sum(e * dp, axis=0, keepdims=True)) * ratio
-            prob = e * ratio
-            p[:, at] = prob.astype(BF16)
-            ds[:, at] = (prob * (dp - delta)).astype(BF16)
-            after[0:1, at] = shrink * ratio
-            after[1:2, at] = delta
-        cols = pl.ds(j * GROUP * HD, GROUP * HD)
-        dk = dot(ds[:, cols], lanes(q, j * GROUP * HD, GROUP)) * SCALE
-        dv = dot(p[:, cols], lanes(do, j * GROUP * HD, GROUP))
-        before[0, :, head] = dk.astype(BF16)
-        before[1, :, head] = dv.astype(BF16)
-
-
-def cross(kv_before, queries, out_grad, stats):
+    seen = jnp.max(stats[3:4, :HD]) == 0.0
+
+    @pl.when(seen)
+    def _():
+        for j in range(features // HD):
+            head = pl.ds(j * HD, HD)
+            k = kv_before[0, :, head]
+            v = kv_before[1, :, head]
+            for h in range(0, GROUP, 2):
+                first = (j * GROUP + h) * HD
+                at = pl.ds(first, CHUNK)
+                top_here, total_here, dot_here = (stats[i : i + 1, at] for i in range(3))
+                logits = dot_t(k, lanes(q, first, 2)) * LOG2_SCALE
+                top = jnp.maximum(jnp.max(logits, axis=0, keepdims=True), top_here)
+                e = jnp.exp2(logits - top)
+                dp = dot_t(v, lanes(do, first, 2))
+                shrink = jnp.exp2(top_here - top)
+                ratio = 1.0 / (total_here * shrink + jnp.sum(e, axis=0, keepdims=True))
+                delta = (dot_here * shrink + jnp.sum(e * dp, axis=0, keepdims=True)) * ratio
+                prob = e * ratio
+                p[:, at] = prob.astype(BF16)
+                ds[:, at] = (prob * (dp - delta)).astype(BF16)
+                after[0:1, at] = shrink * ratio
+                after[1:2, at] = delta
+            cols = pl.ds(j * GROUP * HD, GROUP * HD)
+            dk = dot(ds[:, cols], lanes(q, j * GROUP * HD, GROUP)) * SCALE
+            dv = dot(p[:, cols], lanes(do, j * GROUP * HD, GROUP))
+            before[0, :, head] = dk.astype(BF16)
+            before[1, :, head] = dv.astype(BF16)
+
+    @pl.when(jnp.logical_not(seen))
+    def _():
+        before[...] = jnp.zeros_like(before)
+        p[...] = jnp.zeros_like(p)
+        ds[...] = jnp.zeros_like(ds)
+        ratio = 1.0 / stats[1:2, :]
+        after[0:1, :] = ratio
+        after[1:2, :] = stats[2:3, :] * ratio
+
+
+def cross(kv_before, queries, out_grad, stats, behind):
     _, piece_len, features = kv_before.shape
     width = queries.shape[3]
     return pl.pallas_call(
@@ -375,11 +397,11 @@
             pltpu.VMEM((piece_len, width), BF16),
             pltpu.VMEM((8, width), F32),
         ),
-        in_specs=[in_vmem] * 4,
+        in_specs=[in_vmem] * 5,
         out_specs=(in_vmem,) * 4,
         compiler_params=pltpu.CompilerParams(vmem_limit_bytes=VMEM_LIMIT),
         name="cross",
-    )(kv_before, queries, out_grad, stats)
+    )(kv_before, queries, out_grad, stats, behind)
 
 
 def turn(wide, ref, first):
@@ -387,10 +409,11 @@
         ref[:, pl.ds(first + i * HD, HD)] = wide[:, i * HD : (i + 1) * HD].T
 
 
-def rest_kernel(
-    near_kv, next_kv, queries, out_grad, weights, dprobs, p_next, ds_next, after, passed, far_kv, mate_kv,
-    p_far, ds_far, out, q_grad, k_grad, v_grad, o, dq, p, ds, dk_low, dv_low, sems,
-):
+def rest_kernel(alone, *refs):
+    near_kv, queries, out_grad, weights, dprobs, after, far_kv, mate_kv, p_far, ds_far = refs[:10]
+    if not alone:
+        next_kv, p_next, ds_next = refs[10:13]
+    out, q_grad, own, o, dq, p, ds, sems = refs[-8:]
     near, far = near_slot(), far_slot()
     q, do = queries.at[near, 0], out_grad.at[near, 0]
     kv_heads = near_kv.shape[2] // HD
@@ -400,7 +423,7 @@
     def give_back(side, slot, j):
         cols = pl.ds(j * span, span)
         for n, (a, b) in enumerate(((o, out), (dq, q_grad))):
-            sem = sems.at[2 + (side * kv_heads + j) * 2 + n]
+            sem = sems.at[(side * kv_heads + j) * 2 + n]
             back = pltpu.make_async_copy(a.at[side, :, cols], b.at[slot, 0, :, cols], sem)
             back.start()
             backs.append(back)
@@ -417,113 +440,172 @@
         give_back(1, far, j)
     for j in range(kv_heads):
         head = pl.ds(j * HD, HD)
-        k_t = jnp.concatenate([next_kv[0, :, head], near_kv[0, :, head]], axis=0).T
-        v_t = jnp.concatenate([next_kv[1, :, head], near_kv[1, :, head]], axis=0).T
+        if alone:
+            k_t, v_t = near_kv[0, :, head].T, near_kv[1, :, head].T
+        else:
+            k_t = jnp.concatenate([next_kv[0, :, head], near_kv[0, :, head]], axis=0).T
+            v_t = jnp.concatenate([next_kv[1, :, head], near_kv[1, :, head]], axis=0).T
         for h in range(0, GROUP, 2):
             first = (j * GROUP + h) * HD
             at = pl.ds(first, CHUNK)
-            prob = weights[:, at] * after[0:1, at]
+            if alone:
+                ratio = 1.0 / after[1:2, at]
+                delta = after[2:3, at] * ratio
+            else:
+                ratio, delta = after[0:1, at], after[1:2, at]
+            prob = weights[:, at] * ratio
             prob_low = prob.astype(BF16)
-            ds_low = (prob * (dprobs[:, at] - after[1:2, at])).astype(BF16)
+            ds_low = (prob * (dprobs[:, at] - delta)).astype(BF16)
             p[:, pl.ds(h * HD, CHUNK)] = prob_low
             ds[:, pl.ds(h * HD, CHUNK)] = ds_low
-            turn(dot(v_t, jnp.concatenate([p_next[:, at], prob_low], axis=0)).astype(BF16), o.at[0], first)
-            dq_t = dot(k_t, jnp.concatenate([ds_next[:, at], ds_low], axis=0)) * SCALE
-            turn(dq_t.astype(BF16), dq.at[0], first)
+            if not alone:
+                prob_low = jnp.concatenate([p_next[:, at], prob_low], axis=0)
+                ds_low = jnp.concatenate([ds_next[:, at], ds_low], axis=0)
+            turn(dot(v_t, prob_low).astype(BF16), o.at[0], first)
+            turn((dot(k_t, ds_low) * SCALE).astype(BF16), dq.at[0], first)
         give_back(0, near, j)
-        dk = dot(ds[...], lanes(q, j * span, GROUP)) * SCALE
-        dv = dot(p[...], lanes(do, j * span, GROUP))
-        dk_low[:, head] = (dk + passed[0, :, head].astype(F32)).astype(BF16)
-        dv_low[:, head] = (dv + passed[1, :, head].astype(F32)).astype(BF16)
-    backs += fetch_pairs([(dk_low, k_grad.at[near, 0]), (dv_low, v_grad.at[near, 0])], sems)
+        own[0, :, head] = dot(ds[...], lanes(q, j * span, GROUP)) * SCALE
+        own[1, :, head] = dot(p[...], lanes(do, j * span, GROUP))
     for back in backs:
         back.wait()
 
 
-def rest(*operands, shape):
+def rest(alone, *operands, shape):
     _, piece_len, features = operands[0].shape
     width = shape[3]
     kv_heads = features // HD
-    wide = jax.ShapeDtypeStruct(shape, BF16)
-    small = jax.ShapeDtypeStruct(shape[:3] + (features,), BF16)
+    wide = pltpu.HBM(shape, BF16)
     return pl.pallas_call(
-        rest_kernel,
-        out_shape=(wide, wide, small, small),
+        functools.partial(rest_kernel, alone),
+        out_shape=(wide, wide, pltpu.VMEM((2, piece_len, features), F32)),
         in_specs=[in_vmem] * len(operands),
-        out_specs=(in_hbm,) * 4,
+        out_specs=(in_hbm, in_hbm, in_vmem),
         scratch_shapes=[pltpu.VMEM((2, piece_len, width), BF16)] * 2
         + [pltpu.VMEM((piece_len, GROUP * HD), BF16)] * 2
-        + [pltpu.VMEM((piece_len, features), BF16)] * 2
-        + [pltpu.SemaphoreType.DMA((2 + 4 * kv_heads,))],
+        + [pltpu.SemaphoreType.DMA((4 * kv_heads,))],
         compiler_params=pltpu.CompilerParams(vmem_limit_bytes=VMEM_LIMIT),
         name="rest",
     )(*operands)
 
 
-def total_kernel(own, passed, k_grad_in, v_grad_in, k_grad, v_grad, low, sems):
-    far = far_slot()
-    low[...] = (own[...] + passed[...].astype(F32)).astype(BF16)
-    copies = fetch_pairs([(low.at[0], k_grad.at[far, 0]), (low.at[1], v_grad.at[far, 0])], sems)
-    for copy in copies:
+def total_kernel(near_own, far_own, near_back, *refs):
+    k_grad, v_grad, k_low, v_low, sems = refs[-5:]
+    near, far = near_slot(), far_slot()
+    for n, low in enumerate((k_low, v_low)):
+        low[near, 0] = (near_own[n] + near_back[n].astype(F32)).astype(BF16)
+        mine = far_own[n]
+        if len(refs) > 5:
+            mine = mine + refs[0][n].astype(F32)
+        low[far, 0] = mine.astype(BF16)
+    for copy in fetch_pairs([(k_low, k_grad), (v_low, v_grad)], sems):
         copy.wait()
 
 
-def total(own, passed, k_grad, v_grad):
+def total(*operands):
+    _, piece_len, features = operands[0].shape
+    shape = (2, 1, piece_len, features)
     return pl.pallas_call(
         total_kernel,
-        out_shape=(jax.ShapeDtypeStruct(k_grad.shape, BF16),) * 2,
-        in_specs=[in_vmem] * 2 + [in_hbm] * 2,
+        out_shape=(pltpu.HBM(shape, BF16),) * 2,
+        in_specs=[in_vmem] * len(operands),
         out_specs=(in_hbm,) * 2,
-        input_output_aliases={2: 0, 3: 1},
-        scratch_shapes=[pltpu.VMEM(own.shape, BF16), pltpu.SemaphoreType.DMA((2,))],
+        scratch_shapes=[pltpu.VMEM(shape, BF16)] * 2 + [pltpu.SemaphoreType.DMA((2,))],
         compiler_params=pltpu.CompilerParams(vmem_limit_bytes=VMEM_LIMIT),
         name="total",
-    )(own, passed, k_grad, v_grad)
-
-
-def complete(route, pairs, flip=False):
+    )(*operands)
+
+
+def complete(route, pairs, spare):
+    def whole_turn(routes):
+        ends = [sorted(side) for side in zip(*routes)]
+        return ends == [list(range(pairs))] * 2 and all(a != b for a, b in routes)
+
+    if whole_turn(route + spare):
+        return route + spare
     sources = [i for i in range(pairs) if i not in {a for a, _ in route}]
     targets = [i for i in range(pairs) if i not in {b for _, b in route}]
-    spare = [(i, i ^ 1) for i in sources if i ^ 1 in targets]
-    sources = [i for i in sources if i not in {a for a, _ in spare}]
-    targets = [i for i in targets if i not in {b for _, b in spare}]
-    if flip:
-        targets = targets[::-1]
-    for turn_by in range(max(1, len(targets))):
-        turned = targets[turn_by:] + targets[:turn_by]
-        if all(a != b for a, b in zip(sources, turned)):
-            return route + spare + list(zip(sources, turned))
+    for turn_by in range(len(targets)):
+        filled = route + list(zip(sources, targets[turn_by:] + targets[:turn_by]))
+        if whole_turn(filled):
+            return filled
     return route
 
 
-def local_pairs(queries, keys, values, out_grad, block_doc):
+def far_links(pairs):
+    low = [(i, i + 1, i) for i in range(3, pairs - 1, 2)]
+    high = [(i + 1, i, 2 * pairs - 2 - i) for i in range(1, pairs - 3, 2)]
+    return low + high
+
+
+def is_outer(link):
+    return min(link[0], link[1]) % 4 == 3
+
+
+SPARE = {
+    "both": [(1, 0), (6, 7), (0, 2), (7, 5)],
+    "both back": [(0, 1), (7, 6), (2, 7), (5, 0)],
+    "outer": [(2, 6), (6, 7), (7, 5), (5, 1), (1, 0), (0, 2)],
+    "outer back": [(2, 6), (6, 7), (7, 5), (5, 1), (1, 0), (0, 2)],
+    "inner": [(3, 2), (4, 5), (6, 7), (1, 0), (0, 3), (7, 4)],
+    "inner back": [(2, 3), (5, 4), (7, 6), (0, 1), (3, 0), (4, 7)],
+}
+
+
+def attend_pairs(links, name, queries, out_grad, doc, far_kv, near_kv):
     pairs = lax.axis_size("ctx")
     mates = [(i, i ^ 1) for i in range(pairs) if i ^ 1 < pairs]
-    low_route = [(i, i + 1) for i in range(3, pairs - 1, 2)]
-    high_route = [(i + 1, i) for i in range(1, pairs - 3, 2)]
-    links = low_route + high_route
-    route = complete(links, pairs)
-    route_back = complete([(b, a) for a, b in links], pairs, flip=True)
-    far_kv, near_kv = keep(*pick(keys, values))
+    flows = [(a, b) for a, b, _ in links]
+    far_kv, near_kv = keep(far_kv, near_kv)
     mate_kv = lax.ppermute(near_kv, "ctx", mates)
-    next_kv = lax.ppermute(far_kv, "ctx", route)
-    weights, dprobs, stats = diagonal(block_doc, near_kv, queries, out_grad)
-    mate_grads, own_grads, p_far, ds_far = whole(stats, far_kv, mate_kv, queries, out_grad)
+    if links:
+        next_kv = lax.ppermute(far_kv, "ctx", complete(flows, pairs, SPARE[name]))
+    weights, dprobs, stats = diagonal(doc, near_kv, queries, out_grad)
+    mate_grads, far_own, p_far, ds_far = whole(stats, far_kv, mate_kv, queries, out_grad)
     mate_back = lax.ppermute(mate_grads, "ctx", mates)
-    next_grads, p_next, ds_next, after = cross(next_kv, queries, out_grad, stats)
-    next_back = lax.ppermute(next_grads, "ctx", route_back)
-    out, q_grad, k_grad, v_grad = rest(
-        near_kv, next_kv, queries, out_grad, weights, dprobs, p_next, ds_next, after, mate_back,
-        far_kv, mate_kv, p_far, ds_far, shape=queries.shape,
-    )
-    k_grad, v_grad = total(own_grads, next_back, k_grad, v_grad)
+    after, more, far_back = stats, (), ()
+    if links:
+        next_grads, p_next, ds_next, after = cross(
+            next_kv, queries, out_grad, stats, mate_grads
+        )
+        more = (next_kv, p_next, ds_next)
+        back = [(b, a) for a, b in flows]
+        far_back = (
+            lax.ppermute(next_grads, "ctx", complete(back, pairs, SPARE[name + " back"])),
+        )
+    out, q_grad, near_own = rest(
+        not links, near_kv, queries, out_grad, weights, dprobs, after, far_kv, mate_kv, p_far,
+        ds_far, *more, shape=queries.shape,
+    )
+    k_grad, v_grad = total(near_own, far_own, mate_back, *far_back)
     return (out, q_grad, k_grad, v_grad)
+
+
+def local_pairs(queries, keys, values, out_grad, block_doc):
+    links = far_links(lax.axis_size("ctx"))
+    outer = [link for link in links if is_outer(link)]
+    inner = [link for link in links if not is_outer(link)]
+
+    def needed(doc):
+        def any_linked(some):
+            same = [doc[first] == doc[first + 1] for _, _, first in some]
+            return functools.reduce(jnp.logical_or, same)
+
+        return jnp.where(any_linked(inner), 1, 0) + jnp.where(any_linked(outer), 2, 0)
+
+    far_kv, near_kv, case, doc = pick(keys, values, block_doc, needed)
+    cases = (([], "none"), (inner, "inner"), (outer, "outer"), (links, "both"))
+    return lax.switch(
+        case[0],
+        [functools.partial(attend_pairs, some, name) for some, name in cases],
+        queries, out_grad, doc, far_kv, near_kv,
+    )
 
 
 def local(queries, keys, values, out_grad, block_doc):
     window = min(7, lax.axis_size("ctx") // 4 - 1) + 1
     piece_len = queries.shape[2]
-    if window == 2 and piece_len == BLOCK:
+    even = lax.axis_size("ctx") % 2 == 0
+    if window == 2 and piece_len == BLOCK and even:
         return local_pairs(queries, keys, values, out_grad, block_doc)
     return local_wide(queries, keys, values, out_grad, block_doc)
 

time: 15.9 us -> 13.6 us (0.86)
  the two profiles are of different devices: /device:TPU:27 before, /device:TPU:0 now
where the time goes in v3:
time: 13.6 us; the launch traced here: 13.5 us
  Pallas kernels  6.82 us (50%)
  starting transfers between devices  3.73 us (27%)
  waiting for transfers between devices  1.75 us (13%)
  between operations  0.83 us (6%)
  loops' own time  0.34 us (2%)
    ppermute x1, starting transfers between devices, attend_pairs(): next_kv = lax.ppermute(far_kv, 'ctx', complete(flows, pairs, SPARE[name]))  2.6 us
    pallas_call x1, Pallas kernels, whole(): pl.pallas_call(whole_kernel, out_shape=(pltpu.VMEM((2, piece_len, feature...  2.14 us
    pallas_call x1, Pallas kernels, rest(): pl.pallas_call(functools.partial(rest_kernel, alone), out_shape=(wide, wi...  2.14 us
    ppermute x1, waiting for transfers between devices, attend_pairs(): lax.ppermute(next_grads, 'ctx', complete(back, pairs, SPARE[name + ' back...  1.75 us
    pallas_call x1, Pallas kernels, pick(): pl.pallas_call(functools.partial(pick_kernel, needed), out_shape=(shape,...  0.99 us
    pallas_call x1, Pallas kernels, total(): pl.pallas_call(total_kernel, out_shape=(pltpu.HBM(shape, BF16),) * 2, in_...  0.74 us
    pallas_call x1, Pallas kernels, diagonal(): pl.pallas_call(diagonal_kernel, out_shape=(pltpu.VMEM((piece_len, width),...  0.6 us
    ppermute x1, starting transfers between devices, attend_pairs(): lax.ppermute(next_grads, 'ctx', complete(back, pairs, SPARE[name + ' back...  0.54 us
  transfers between devices with their start and end apart: 4, of which 1 were waited for; matrix products, arithmetic and copies ran while one was open for 0% of the time, Pallas kernels for 38%

profile of v3, /device:TPU:0, one launch (start us, length us, event | category | flops | bytes accessed | tf_op | source)
XLA Modules:
  0.0 13.5 jit_solution(11107506511864762964)
XLA Ops:
  0.6 1.0 %pick.1 = (bf16[2,128,256]{2,1,0:T(8,128)(2,1)S(1)}, bf16[2,128,256]{2,1,0:T(8,128)(2,1)S(1)}, s32[1]{0:T(128)S(4)}, s32[16]{0:T(128)S(4)}) custom-call(bf16[2,1,128,256]{3,2,1,0:T(8,128)(2,1)} %keys.1, bf16[2,1,128,256]{3,2,1,0:T(8,128)(2,1)} %values.1, s32[16]{0:T(128)} %block_doc.1), custom_call_target="tpu_custom_call" | custom-call | tf_op jit(solution)/shard_map/pick/pallas_call | solution.py:216
  1.6 11.7 %conditional.1 = (bf16[2,1,128,2048]{3,2,1,0:T(8,128)(2,1)}, bf16[2,1,128,2048]{3,2,1,0:T(8,128)(2,1)}, bf16[2,1,128,256]{3,2,1,0:T(8,128)(2,1)}, bf16[2,1,128,256]{3,2,1,0:T(8,128)(2,1)}) conditional(s32[]{:T(128)} %bitcast, (bf16[2,128,256]{2,1,0:T(8,128)(2,1)S(1)}, bf16[2,128,256]{2,1,0:T(8,128)(2,1)S(1)}, ...), branch_computations={%region_0.0_spmd, %region_1.0_spmd, %region_2.0_spmd, %region_3.0_... | conditional | flops 10000000000 | bytes 11486008 | solution.py:597
  1.7 0.0 copy-start.1
  1.7 0.0 copy-start.5
  1.7 0.5 %collective-permute-start.3 = (bf16[2,128,256]{2,1,0:T(8,128)(2,1)S(1)}, bf16[2,128,256]{2,1,0:T(8,128)(2,1)S(1)}, u32[]{:S(2)}, u32[]{:S(2)}) collective-permute-start(bf16[2,128,256]{2,1,0:T(8,128)(2,1)S(1)} %get-tuple-element.61.kv.refs_0_), channel_id=1, source_target_pairs={{0,4},{4,0},{8,12},{12,8},{16,20},{20,16},{24,28},{28,24},{1,5},{5... | collective-permute-start | bytes 393224 | tf_op jit(solution)/shard_map/cond/branch_1_fun/ppermute | solution.py:559
  2.2 2.6 %collective-permute-start.2 = (bf16[2,128,256]{2,1,0:T(8,128)(2,1)S(1)}, bf16[2,128,256]{2,1,0:T(8,128)(2,1)S(1)}, u32[]{:S(2)}, u32[]{:S(2)}) collective-permute-start(bf16[2,128,256]{2,1,0:T(8,128)(2,1)S(1)} %get-tuple-element.67.kv.refs_6_), channel_id=1, source_target_pairs={{20,24},{8,4},{12,8},{16,20},{24,28},{4,0},{0,12},{28,16},{21,25},... | collective-permute-start | bytes 393224 | tf_op jit(solution)/shard_map/cond/branch_1_fun/ppermute | solution.py:561
  4.8 0.0 copy-done.1
  4.8 0.0 copy-done.5
  4.8 0.6 %diagonal.5 = (f32[128,2048]{1,0:T(8,128)S(1)}, f32[128,2048]{1,0:T(8,128)S(1)}, f32[8,2048]{1,0:T(8,128)S(1)}) custom-call(s32[16]{0:T(128)S(4)} %get-tuple-element.64.doc, bf16[2,128,256]{2,1,0:T(8,128)(2,1)S(1)} %get-tuple-element.61.kv.refs_0_, bf16[2,1,128,2048]{3,2,1,0:T(8,128)(2,1)S(1)} %copy-done.1, bf16[2,1,128,2048]{3,2,1,0:T(8,128)(2,1)S(1)} %copy-done.5), custom_call_target="tpu_custom_call" | custom-call | tf_op jit(solution)/shard_map/cond/branch_1_fun/diagonal/pallas_call | solution.py:277
  5.4 0.0 collective-permute-done.3.kv_before.refs_7_
  5.4 2.1 %whole.5 = (bf16[2,128,256]{2,1,0:T(8,128)(2,1)S(1)}, f32[2,128,256]{2,1,0:T(8,128)S(1)}, bf16[256,2048]{1,0:T(8,128)(2,1)S(1)}, bf16[256,2048]{1,0:T(8,128)(2,1)S(1)}) custom-call(f32[8,2048]{1,0:T(8,128)S(1)} %get-tuple-element.68.stats, bf16[2,128,256]{2,1,0:T(8,128)(2,1)S(1)} %get-tuple-element.67.kv.refs_6_, ...), custom_call_target="tpu_custom_call" | custom-call | tf_op jit(solution)/shard_map/cond/branch_1_fun/whole/pallas_call | solution.py:330
  7.6 0.1 collective-permute-start.4
  7.7 0.0 collective-permute-done.2.kv_before.refs_10_
  7.7 0.2 %cross.3 = (bf16[2,128,256]{2,1,0:T(8,128)(2,1)S(1)}, bf16[128,2048]{1,0:T(8,128)(2,1)S(1)}, bf16[128,2048]{1,0:T(8,128)(2,1)S(1)}, f32[8,2048]{1,0:T(8,128)S(1)}) custom-call(bf16[2,128,256]{2,1,0:T(8,128)(2,1)S(1)} %collective-permute-done.2.kv_before.refs_10_, bf16[2,1,128,2048]{3,2,1,0:T(8,128)(2,1)S(1)} %copy-done.1, ...), custom_call_target="tpu_custom_call" | custom-call | tf_op jit(solution)/shard_map/cond/branch_1_fun/cross/pallas_call | solution.py:392
  7.9 0.5 %collective-permute-start.5 = (bf16[2,128,256]{2,1,0:T(8,128)(2,1)S(1)}, bf16[2,128,256]{2,1,0:T(8,128)(2,1)S(1)}, u32[]{:S(2)}, u32[]{:S(2)}) collective-permute-start(bf16[2,128,256]{2,1,0:T(8,128)(2,1)S(1)} %get-tuple-element.79), channel_id=1, source_target_pairs={{24,20},{4,8},{8,12},{20,16},{28,24},{0,4},{12,0},{16,28},{25,21},... | collective-permute-start | bytes 393224 | tf_op jit(solution)/shard_map/cond/branch_1_fun/ppermute | solution.py:573
  8.4 2.1 %rest.5 = (bf16[2,1,128,2048]{3,2,1,0:T(8,128)(2,1)}, bf16[2,1,128,2048]{3,2,1,0:T(8,128)(2,1)}, f32[2,128,256]{2,1,0:T(8,128)S(1)}) custom-call(bf16[2,128,256]{2,1,0:T(8,128)(2,1)S(1)} %get-tuple-element.61.kv.refs_0_, bf16[2,1,128,2048]{3,2,1,0:T(8,128)(2,1)S(1)} %copy-done.1, bf16[2,1,128,2048]{3,2,1,0:T(8,128)(2,1)S(1)} %copy-done.5, ...), custom_call_target="tpu_custom_call" | custom-call | tf_op jit(solution)/shard_map/cond/branch_1_fun/rest/pallas_call | solution.py:478
  10.6 0.0 collective-permute-done.4.near_back
  10.6 1.7 %collective-permute-done.5.refs_0_ = bf16[2,128,256]{2,1,0:T(8,128)(2,1)S(1)} collective-permute-done((bf16[2,128,256]{2,1,0:T(8,128)(2,1)S(1)}, bf16[2,128,256]{2,1,0:T(8,128)(2,1)S(1)}, u32[]{:S(2)}, u32[]{:S(2)}) %collective-permute-start.5) | collective-permute-done | bytes 131104 | tf_op jit(solution)/shard_map/cond/branch_1_fun/ppermute | solution.py:573
  12.3 0.7 %total.5 = (bf16[2,1,128,256]{3,2,1,0:T(8,128)(2,1)}, bf16[2,1,128,256]{3,2,1,0:T(8,128)(2,1)}) custom-call(f32[2,128,256]{2,1,0:T(8,128)S(1)} %get-tuple-element.77.near_own, f32[2,128,256]{2,1,0:T(8,128)S(1)} %get-tuple-element.78.far_own, bf16[2,128,256]{2,1,0:T(8,128)(2,1)S(1)} %collective-permute-done.4.near_back, ...), custom_call_target="tpu_custom_call" | custom-call | tf_op jit(solution)/shard_map/cond/branch_1_fun/total/pallas_call | solution.py:507
  (1 shorter events, 0.0 us)
Async XLA Ops:
  1.7 3.2 %copy-start.1 = (bf16[2,1,128,2048]{3,2,1,0:T(8,128)(2,1)S(1)}, bf16[2,1,128,2048]{3,2,1,0:T(8,128)(2,1)}, u32[]{:S(2)}) copy-start(bf16[2,1,128,2048]{3,2,1,0:T(8,128)(2,1)} %get-tuple-element.62.queries.refs_1_) | copy-start | bytes 3145732 | tf_op jit(solution)/shard_map/cond
  1.7 3.1 %copy-start.5 = (bf16[2,1,128,2048]{3,2,1,0:T(8,128)(2,1)S(1)}, bf16[2,1,128,2048]{3,2,1,0:T(8,128)(2,1)}, u32[]{:S(2)}) copy-start(bf16[2,1,128,2048]{3,2,1,0:T(8,128)(2,1)} %get-tuple-element.63.out_grad.refs_2_) | copy-start | bytes 3145732 | tf_op jit(solution)/shard_map/cond
  1.7 3.7 %collective-permute-start.3 = (bf16[2,128,256]{2,1,0:T(8,128)(2,1)S(1)}, bf16[2,128,256]{2,1,0:T(8,128)(2,1)S(1)}, u32[]{:S(2)}, u32[]{:S(2)}) collective-permute-start(bf16[2,128,256]{2,1,0:T(8,128)(2,1)S(1)} %get-tuple-element.61.kv.refs_0_), channel_id=1, source_target_pairs={{0,4},{4,0},{8,12},{12,8},{16,20},{20,16},{24,28},{28,24},{1,5},{5... | collective-permute-start | bytes 393224 | tf_op jit(solution)/shard_map/cond/branch_1_fun/ppermute | solution.py:559
  2.2 5.5 %collective-permute-start.2 = (bf16[2,128,256]{2,1,0:T(8,128)(2,1)S(1)}, bf16[2,128,256]{2,1,0:T(8,128)(2,1)S(1)}, u32[]{:S(2)}, u32[]{:S(2)}) collective-permute-start(bf16[2,128,256]{2,1,0:T(8,128)(2,1)S(1)} %get-tuple-element.67.kv.refs_6_), channel_id=1, source_target_pairs={{20,24},{8,4},{12,8},{16,20},{24,28},{4,0},{0,12},{28,16},{21,25},... | collective-permute-start | bytes 393224 | tf_op jit(solution)/shard_map/cond/branch_1_fun/ppermute | solution.py:561
  7.6 3.0 %collective-permute-start.4 = (bf16[2,128,256]{2,1,0:T(8,128)(2,1)S(1)}, bf16[2,128,256]{2,1,0:T(8,128)(2,1)S(1)}, u32[]{:S(2)}, u32[]{:S(2)}) collective-permute-start(bf16[2,128,256]{2,1,0:T(8,128)(2,1)S(1)} %get-tuple-element.69.behind), channel_id=1, source_target_pairs={{0,4},{4,0},{8,12},{12,8},{16,20},{20,16},{24,28},{28,24},{1,5},{5... | collective-permute-start | bytes 393224 | tf_op jit(solution)/shard_map/cond/branch_1_fun/ppermute | solution.py:564
  7.9 4.4 %collective-permute-start.5 = (bf16[2,128,256]{2,1,0:T(8,128)(2,1)S(1)}, bf16[2,128,256]{2,1,0:T(8,128)(2,1)S(1)}, u32[]{:S(2)}, u32[]{:S(2)}) collective-permute-start(bf16[2,128,256]{2,1,0:T(8,128)(2,1)S(1)} %get-tuple-element.79), channel_id=1, source_target_pairs={{24,20},{4,8},{8,12},{20,16},{28,24},{0,4},{12,0},{16,28},{25,21},... | collective-permute-start | bytes 393224 | tf_op jit(solution)/shard_map/cond/branch_1_fun/ppermute | solution.py:573
